TPU v7x, 32 devices: a whole 2x2x4 slice. The times are simulated.
32 devices in a mesh: grp: 2 (over y), blk: 8 (over z, x), pair: 2 (over core).
Axes of the slice: x: 2, y: 2, z: 4, core: 2. Of those that a mesh axis runs over, the one named last changes fastest.
Arguments:
- wavefunc: bfloat16 [96, 16, 2, 768], P(('grp', 'blk')), parts along dimension 0, may hold values from -6 to 6
- haydock: float32 [96, 128], P(('grp', 'blk')), parts along dimension 0, may hold values from -6 to 6
- screened: bfloat16 [16, 768, 768], P(('grp', 'blk')), parts along dimension 0, may hold values from -0.21875 to 0.21875
- coulomb: float32 [1536], P('grp'), parts along dimension 0, may hold values from 0.05 to 1
- umklapp_map: int32 [3, 768], replicated, may hold values from 0 to 767, each once within a row
Outputs:
- kernel_out: float32 [96, 128], P(('grp', 'blk')), parts along dimension 0
There are 2 independent parts, one for each index of `grp`. A program takes and returns all parts, laid end to end along the dimension named above; an argument that names none is the same for every part. Nothing has to cross between parts.
Inputs may be any that keep to these rules, and one draw needn't show every extreme that they name: Each row of umklapp_map is a permutation of 0 .. 767.
All inputs are finite; a program needn't handle non-finite values.
Results may differ from a plain program's by a relative error of at most 0.015.
Values may be sent and summed in bfloat16 or wider, within the bound.
No kernel may reach another device: no remote copies, remote signals or barrier semaphores. Data moves between devices by JAX's collectives and lax.ppermute only.
A program may use at most 64 MiB of HBM per device.

v0:
```python
import functools
import math

import jax
import jax.numpy as jnp
from jax import lax
from jax.experimental import pallas as pl
from jax.experimental.pallas import tpu as pltpu
from jax.sharding import PartitionSpec as P

NV = 8
NC = 8
STOPS = 2
BF = jnp.bfloat16
F32 = jnp.float32

BLOCKS = 8
OFFSET = {0: 0, 4: 0, 1: 1, 5: 1, 2: 2, 3: 2}
TARGETS = {
    (0, 0): (0, 1), (0, 1): (2, 3),
    (1, 0): (1, 0), (1, 1): (3, 2),
    (2, 0): (2, 0), (2, 1): (6, 4),
    (3, 0): (3, 1), (3, 1): (7, 5),
    (4, 0): (4, 5), (4, 1): (7, 6),
    (5, 0): (5, 4), (5, 1): (6, 7),
}
MATRIX_MOVES = ((0, 4), (1, 5), (2, 3))
FETCH = {
    (0, 0): (1, None), (0, 1): (2, 3),
    (1, 0): (0, 7), (1, 1): (3, 2),
    (2, 0): (None, 0), (2, 1): (6, 4),
    (3, 0): (None, 1), (3, 1): (7, 5),
    (4, 0): (5, None), (4, 1): (6, 7),
    (5, 0): (4, 3), (5, 1): (7, 6),
}
SUMS = ((0, 4), (4, 0))


def pick_cores(pairs, fixed):
    taken, out = {}, []
    for src, dst in pairs:
        chip, core = (src, dst[1]) if fixed == "dst" else (dst, src[1])
        used = taken.setdefault(chip, set())
        core = core if core not in used else 1 - core
        assert core not in used
        used.add(core)
        a, b = ((chip, core), dst) if fixed == "dst" else (src, (chip, core))
        out.append((a[0] * 2 + a[1], b[0] * 2 + b[1]))
    return out


def plan():
    fetch = [pick_cores([(got[r], at) for at, got in FETCH.items() if got[r] is not None], "dst") for r in range(2)]
    home = [
        pick_cores([(at, t[1] if at[1] == 0 else t[0]) for at, t in TARGETS.items()], "src"),
        pick_cores([(at, t[1]) for at, t in TARGETS.items() if at[1] == 1], "src"),
    ]
    table = {}
    for chip, core in TARGETS:
        first, second = FETCH[chip, core]
        held = [chip, first, FETCH[chip, 1 - core][0], second]
        off = OFFSET[chip]
        moved = int(any(d == chip for _, d in MATRIX_MOVES))
        row = [1, off, moved, int(off == 0)]
        row += [held.index(t) for t in TARGETS[chip, core]]
        row += [held.index((t - off) % BLOCKS) for t in TARGETS[chip, core]]
        table[chip, core] = row
    return fetch, home, table


FETCH_ROUNDS, HOME_ROUNDS, TABLE = plan()


def entry(who, column):
    value = jnp.int32(0)
    for b in range(BLOCKS):
        if (b, 0) in TABLE and (TABLE[b, 0][column] or TABLE[b, 1][column]):
            here = jnp.where(who[1] == 0, TABLE[b, 0][column], TABLE[b, 1][column])
            value = jnp.where(who[0] == b, here, value)
    return value


def iota(shape, dim):
    return lax.broadcasted_iota(jnp.int32, shape, dim)


def one(cond, sign=None):
    hit = jnp.where(cond, 1.0, 0.0)
    return hit if sign is None else hit * sign


def dot(a, b, dims=((1,), (0,)), **kw):
    return lax.dot_general(a, b, (dims, ((), ())), preferred_element_type=F32, **kw)


def message_kernel(flat, hay, mine):
    rows, planes = flat.shape
    kr = hay.shape[0]
    mine[0:rows, :] = flat[...]
    h = hay[...]
    hi = h.astype(BF)
    lo = (h - hi.astype(F32)).astype(BF)
    both = jnp.concatenate([hi.astype(F32), lo.astype(F32)], axis=1)
    mine[rows : rows + 16, :] = jnp.zeros((16, planes), BF)
    mine[rows : rows + 16, 0:256] = jnp.concatenate([both, jnp.zeros((16 - kr, 256), F32)], axis=0).astype(BF)


def perm_kernel(who, umk, screened, perm, w_half):
    planes = perm.shape[0]
    gh = w_half.shape[0]
    w_half[...] = screened[pl.ds(pl.multiple_of(who[1] * gh, 128), gh), :]
    row = umk[pl.ds(entry(who, 1), 1), :]
    perm[...] = one(iota((planes, planes), 0) == row).astype(BF)


def amplitude(msg, v, c):
    rows = v.shape[0]
    for k in range(rows // 16):
        v[16 * k : 16 * k + 16, :] = msg[32 * k : 32 * k + 16, :]
        c[16 * k : 16 * k + 16, :] = msg[32 * k + 16 : 32 * k + 32, :]
    spread = one(iota((rows, 16), 1) == iota((rows, 16), 0) // 16).astype(BF)
    keep = (iota((rows, 256), 1) % 8) == ((iota((rows, 256), 0) // 2) % 8)
    a = iota((128, rows), 0)
    b = iota((128, rows), 1)
    same_v = ((a // 8) % 8) == ((b // 2) % 8)
    part_a, part_b = a // 64, b % 2
    q0 = one(same_v & (part_a == part_b), jnp.where(part_a == 1, -1.0, 1.0))
    q1 = one(same_v & (part_a != part_b))
    q = jnp.concatenate([q0, q1], axis=1).astype(BF)
    block = (iota((rows, rows), 0) // 16) == (iota((rows, rows), 1) // 16)
    real_row = (iota((rows, rows), 0) % 2) == 0
    x = jnp.where(keep, dot(spread, msg[2 * rows : 2 * rows + 16, 0:256]), 0.0).astype(BF)
    pieces = []
    for piece in (x[:, 0:128], x[:, 128:256]):
        y = dot(piece, q)
        y0, y1 = y[:, :rows], y[:, rows:]
        pieces.append(jnp.where(block, jnp.where(real_row, y0, y1), 0.0).astype(BF))
        pieces.append(jnp.where(block, jnp.where(real_row, y1, -y0), 0.0).astype(BF))
    bands = v[...]
    return dot(pieces[0], bands) + dot(pieces[2], bands), dot(pieces[1], bands) + dot(pieces[3], bands)


def sums(c, amp, turned):
    cf = c[...].astype(F32)
    return jnp.concatenate([jnp.sum(cf * amp, axis=0, keepdims=True), jnp.sum(cf * turned, axis=0, keepdims=True)], axis=0)


def turn_matrix(rows):
    rr, cc = iota((rows, rows), 0), iota((rows, rows), 1)
    pairs = one(rr == (cc + 1 - 2 * (cc % 2)))
    return jnp.where(rr % 2 == 0, pairs, -pairs).astype(BF)


def permute(a, c, perm, ap_refs, wt_refs, cb_refs):
    n = len(ap_refs)
    rows = c.shape[0] // n
    turn = turn_matrix(rows)
    wp = dot(c[...], perm[...])
    ap = dot(a[...], perm[...]).astype(BF)
    for j in range(n):
        part = slice(j * rows, (j + 1) * rows)
        ap_refs[j][0:rows, :] = ap[part]
        ap_refs[j][rows : 2 * rows, :] = dot(turn, ap[part]).astype(BF)
        wt_refs[j][...] = jnp.transpose(wp[part]).astype(BF)
        cb_refs[j][...] = (-dot(turn, c[part, :])).astype(BF)


def prep_kernel(n, who, perm, *refs):
    msgs, (ap, wt, v, ca, cb, xs, a_scr) = refs[:n], refs[n:]
    rows, planes = v.shape[1:]

    @pl.when(entry(who, 0) == 1)
    def _():
        total = jnp.zeros((2, planes), F32)
        for j in range(n):
            mine = pl.ds(j * rows, rows)
            amp, turned = amplitude(msgs[j], v.at[j], ca.at[mine])
            total = total + sums(ca.at[mine], amp, turned)
            a_scr[mine, :] = amp.astype(BF)
        xs[...] = total
        each = range(n)
        permute(a_scr, ca, perm, [ap.at[j] for j in each], [wt.at[j] for j in each], [cb.at[j] for j in each])

    @pl.when(entry(who, 0) == 0)
    def _():
        xs[...] = jnp.zeros_like(xs)


def last_kernel(who, msg, xs_0, xs_1, v, c, a, xs):
    @pl.when(entry(who, 0) == 1)
    def _():
        amp, turned = amplitude(msg, v, c)
        a[...] = amp.astype(BF)
        xs[...] = xs_0[...] + xs_1[...] + sums(c, amp, turned)

    @pl.when(entry(who, 0) == 0)
    def _():
        xs[...] = jnp.zeros_like(xs)


def main_kernel(who, perm, w_own, w_in, w_swapped, *refs):
    own, two, (v_3, c_3, a_3) = refs[0:5], refs[5:10], refs[10:13]
    d_ref, vt_ref, ca_ref, cb_ref, wf, ap_3, wt_3, cb_3, ap_scr, wt_scr = refs[13:]
    rows, planes = v_3.shape
    gh = planes // 2
    p = who[1]

    @pl.when((entry(who, 0) == 1) & (entry(who, 2) == 0))
    def _():
        wf[...] = w_own[...].astype(F32)

    @pl.when((entry(who, 0) == 1) & (entry(who, 2) == 1))
    def _():
        wf[pl.ds(pl.multiple_of(p * gh, 128), gh), :] = w_in[...].astype(F32)
        wf[pl.ds(pl.multiple_of((1 - p) * gh, 128), gh), :] = w_swapped[...].astype(F32)

    @pl.when(entry(who, 0) == 1)
    def _():
        permute(a_3, c_3, perm, [ap_3], [wt_3], [cb_3])

    def held(slot):
        if slot == 3:
            return ap_3, wt_3, v_3, c_3, cb_3
        ap, wt, v, ca, cb = own if slot == 0 else two
        j = max(slot - 1, 0)
        return ap.at[j], wt.at[j], v.at[j], ca.at[pl.ds(j * rows, rows)], cb.at[j]

    for i in range(2):
        for slot in range(4):

            @pl.when((entry(who, 0) == 1) & (entry(who, 4 + i) == slot))
            def _(i=i, slot=slot):
                _, _, v, ca, cb = held(slot)
                vt_ref[i], ca_ref[i], cb_ref[i] = v[...], ca[...], cb[...]

            @pl.when((entry(who, 0) == 1) & (entry(who, 6 + i) == slot))
            def _(i=i, slot=slot):
                ap, wt = held(slot)[:2]
                ap_scr[i], wt_scr[i] = ap[...], wt[...]

    @pl.when(entry(who, 0) == 1)
    def _():
        kernels = []
        for i in range(2):
            for h in range(2):
                w = wf[h * gh : (h + 1) * gh, :]
                left = wt_scr[i, h * gh : (h + 1) * gh, :]
                k_re = (w * dot(left, ap_scr[i, 0:rows, :])).astype(BF)
                k_im = (w * dot(left, ap_scr[i, rows : 2 * rows, :])).astype(BF)
                kernels.append((k_re, k_im))
        sides = []
        for i in range(2):
            y = None
            for h in range(2):
                k_re, k_im = kernels[2 * i + h]
                part = slice(h * gh, (h + 1) * gh)
                z = dot(ca_ref[i, :, part], k_re) + dot(cb_ref[i, :, part], k_im)
                y = z if y is None else y + z
            sides.append(y.astype(BF))
        for i, y in enumerate(sides):
            d_ref[i] = dot(y, vt_ref[i], ((1,), (1,)))


def finish_kernel(scale_direct, scale_exchange, who, d_ref, v, ca, cb, *refs):
    xs, xs_swapped, xs_in, xs_in_swapped, coulomb, stays, goes_1, goes_2 = refs
    rows = v.shape[1]
    kr = rows // 16
    p = who[1]
    a = iota((rows, 128), 0)
    b = iota((rows, 128), 1)
    same_v = ((a // 2) % 8) == ((b // 8) % 8)
    ra, rb = a % 2, b // 64
    qa = one(same_v & (ra == rb), jnp.where(rb == 1, -1.0, 1.0))
    qb = one(same_v & (ra != rb))
    q = jnp.concatenate([qa, qb], axis=1)
    real_row = (a % 2) == 0
    keep = (b % 8) == ((a // 2) % 8)
    block = (iota((rows, rows), 0) // 16) == (iota((rows, rows), 1) // 16)

    def result(d):
        d = jnp.where(block, d, 0.0)
        z = dot(d, q, precision=lax.Precision.HIGHEST)
        z = jnp.where(keep, jnp.where(real_row, z[:, :128], z[:, 128:]), 0.0)
        return jnp.sum(z.reshape(kr, 16, 128), axis=1)

    def store(one_, two):
        r1, r2 = result(one_), result(two)
        core_0 = p == 0
        stays[...] = jnp.where(core_0, r1, 0.0)
        goes_1[...] = jnp.where(core_0, r2, r1)
        goes_2[...] = jnp.where(core_0, 0.0, r2)

    @pl.when(entry(who, 0) == 0)
    def _():
        for o in (stays, goes_1, goes_2):
            o[...] = jnp.zeros_like(o)

    @pl.when((entry(who, 0) == 1) & (entry(who, 3) == 0))
    def _():
        store(*(d_ref[i] * scale_direct for i in range(2)))

    @pl.when((entry(who, 0) == 1) & (entry(who, 3) == 1))
    def _():
        total = jnp.where(p == 1, xs[...] + xs_in[...], xs_swapped[...] + xs_in_swapped[...])
        y = coulomb[...] * total * scale_exchange
        both = []
        for i in range(2):
            side = (ca[i].astype(F32) * y[0:1] + cb[i].astype(F32) * y[1:2]).astype(BF)
            both.append(d_ref[i] * scale_direct + dot(side, v[i], ((1,), (1,))))
        store(*both)


VM = pl.BlockSpec(memory_space=pltpu.VMEM)
SM = pl.BlockSpec(memory_space=pltpu.SMEM)


def call(kernel, outs, ins, scratch=(), limit=24 << 20):
    moved = sum(math.prod(x.shape) * x.dtype.itemsize for x in (*ins, *outs))
    specs = [SM if x.dtype == jnp.int32 and x.ndim == 1 else VM for x in ins]
    return pl.pallas_call(
        kernel,
        out_shape=outs,
        in_specs=specs,
        out_specs=[VM] * len(outs),
        scratch_shapes=list(scratch),
        compiler_params=pltpu.CompilerParams(vmem_limit_bytes=limit),
        cost_estimate=pl.CostEstimate(flops=0, bytes_accessed=moved, transcendentals=0),
    )(*ins)


def eight_blocks(wavefunc, haydock, screened, coulomb, umklapp_map):
    kr, nb, _, planes = wavefunc.shape
    rows = kr * 16
    gh = planes // 2
    shape = jax.ShapeDtypeStruct
    member = lax.axis_index("pair").astype(jnp.int32)
    who = jnp.stack([lax.axis_index("blk").astype(jnp.int32), member])

    def over_cores(x, pairs):
        return lax.ppermute(x, ("blk", "pair"), pairs)

    def swap(x):
        return lax.ppermute(x, "pair", [(0, 1), (1, 0)])

    def prep(perm, msgs):
        n = len(msgs)
        outs = [
            shape((n, 2 * rows, planes), BF),
            shape((n, planes, rows), BF),
            shape((n, rows, planes), BF),
            shape((n * rows, planes), BF),
            shape((n, rows, planes), BF),
            shape((2, planes), F32),
        ]
        return call(
            functools.partial(prep_kernel, n), outs, [who, perm, *msgs], scratch=[pltpu.VMEM((n * rows, planes), BF)]
        )

    flat = wavefunc.reshape(kr * nb * 2, planes)
    perm, w_half = call(
        perm_kernel, [shape((planes, planes), BF), shape((gh, planes), BF)], [who, umklapp_map, screened[0]]
    )
    w_in = lax.ppermute(w_half, "blk", MATRIX_MOVES)
    (mine,) = call(message_kernel, [shape((2 * rows + 16, planes), BF)], [flat, haydock])
    got_1 = over_cores(mine, FETCH_ROUNDS[0])
    own = prep(perm, [mine])
    got_1, mine, *own = lax.optimization_barrier((got_1, mine, *own))
    got_2 = over_cores(mine, FETCH_ROUNDS[1])
    two = prep(perm, [got_1, swap(got_1)])
    got_2, w_in, *two = lax.optimization_barrier((got_2, w_in, *two))
    bands = shape((rows, planes), BF)
    v_3, c_3, a_3, xs = call(
        last_kernel, [bands, bands, bands, shape((2, planes), F32)], [who, got_2, own[5], two[5]]
    )
    xs_in = lax.ppermute(xs, "blk", SUMS)
    xs_all = [xs, swap(xs), xs_in, swap(xs_in)]
    total_k = kr * lax.axis_size("blk")
    scale_exchange = 1.0 / (8.0 * math.sqrt(planes * total_k))
    scale_direct = -1.0 / (8.0 * math.sqrt(planes * kr * (STOPS + 1)))
    item = shape((2, rows, planes), BF)
    d, v, ca, cb = call(
        main_kernel,
        [shape((2, rows, rows), F32), item, item, item],
        [who, perm, screened[0], w_in, swap(w_in), *own[:5], *two[:5], v_3, c_3, a_3],
        scratch=[
            pltpu.VMEM((planes, planes), F32),
            pltpu.VMEM((2 * rows, planes), BF),
            pltpu.VMEM((planes, rows), BF),
            pltpu.VMEM((rows, planes), BF),
            pltpu.VMEM((2, 2 * rows, planes), BF),
            pltpu.VMEM((2, planes, rows), BF),
        ],
    )
    stays, goes_1, goes_2 = call(
        functools.partial(finish_kernel, scale_direct, scale_exchange),
        [shape((kr, 128), F32)] * 3,
        [who, d, v, ca, cb, *xs_all, coulomb.reshape(1, planes)],
    )
    total = stays + over_cores(goes_1, HOME_ROUNDS[0]) + over_cores(goes_2, HOME_ROUNDS[1])
    return total + swap(total)


def from_root(block, axis, holder):
    block = jnp.where(lax.axis_index(axis) == holder, block, jnp.zeros_like(block))
    return lax.psum(block, axis)


def from_behind(value, axis, by):
    devices = lax.axis_size(axis)
    return lax.ppermute(value, axis, [(i, (i + by) % devices) for i in range(devices)])


def make_amplitude(wave_rows, amp_rows):
    count = wave_rows.shape[0]
    valence = wave_rows[:, :NV].astype(jnp.float32)
    val_re = valence[:, :, 0]
    val_im = valence[:, :, 1]
    amps = amp_rows.reshape(count, 2, NV, NC)
    amp_re = amps[:, 0]
    amp_im = amps[:, 1]
    out_re = jnp.einsum("kvg,kvc->kcg", val_re, amp_re) - jnp.einsum("kvg,kvc->kcg", val_im, amp_im)
    out_im = jnp.einsum("kvg,kvc->kcg", val_re, amp_im) + jnp.einsum("kvg,kvc->kcg", val_im, amp_re)
    return jnp.stack([out_re, out_im], axis=2).astype(jnp.bfloat16)


def densities(wave_rows):
    wide = wave_rows.astype(jnp.float32)
    val_re = wide[:, :NV, 0][:, :, None, :]
    val_im = wide[:, :NV, 1][:, :, None, :]
    cond_re = wide[:, NV:, 0][:, None, :, :]
    cond_im = wide[:, NV:, 1][:, None, :, :]
    return (val_re * cond_re + val_im * cond_im, val_re * cond_im - val_im * cond_re)


def fold_exchange(dens_re, dens_im, amp_rows):
    count = amp_rows.shape[0]
    amps = amp_rows.reshape(count, 2, NV, NC)
    amp_re = amps[:, 0]
    amp_im = amps[:, 1]
    x_re = jnp.einsum("kvcg,kvc->g", dens_re, amp_re) + jnp.einsum("kvcg,kvc->g", dens_im, amp_im)
    x_im = jnp.einsum("kvcg,kvc->g", dens_re, amp_im) - jnp.einsum("kvcg,kvc->g", dens_im, amp_re)
    return (x_re, x_im)


def exchange_terms(dens_re, dens_im, x_re, x_im, coulomb):
    count = dens_re.shape[0]
    y_re = coulomb * x_re
    y_im = coulomb * x_im
    out_re = jnp.einsum("kvcg,g->kvc", dens_re, y_re) - jnp.einsum("kvcg,g->kvc", dens_im, y_im)
    out_im = jnp.einsum("kvcg,g->kvc", dens_re, y_im) + jnp.einsum("kvcg,g->kvc", dens_im, y_re)
    return jnp.stack([out_re, out_im], axis=1).reshape(count, -1)


def direct_fold(wave_rows, permuted, weight):
    valence = wave_rows[:, :NV].astype(jnp.float32)
    val_re = valence[:, :, 0][:, None, :, None, :]
    val_im = valence[:, :, 1][:, None, :, None, :]
    wide = permuted.astype(jnp.float32)
    ahat_re = wide[:, :NC, 0][None, :, None, :, :]
    ahat_im = wide[:, :NC, 1][None, :, None, :, :]
    cond_re = wide[:, NC:, 0]
    cond_im = wide[:, NC:, 1]
    y_re = val_re * ahat_re + val_im * ahat_im
    y_im = val_re * ahat_im - val_im * ahat_re
    stacked = jnp.stack([y_re, y_im], axis=4).astype(jnp.bfloat16)
    flat = stacked.reshape(-1, weight.shape[1])
    image = lax.dot_general(flat, weight, (((1,), (1,)), ((), ())), preferred_element_type=jnp.float32)
    image = image.reshape(stacked.shape)
    z_re = image[:, :, :, :, 0]
    z_im = image[:, :, :, :, 1]
    e_re = jnp.einsum("kjvcg,jcg->kvg", z_re, cond_re) + jnp.einsum("kjvcg,jcg->kvg", z_im, cond_im)
    e_im = jnp.einsum("kjvcg,jcg->kvg", z_im, cond_re) - jnp.einsum("kjvcg,jcg->kvg", z_re, cond_im)
    return (e_re, e_im)


def finish_direct(wave_rows, e_re, e_im):
    count = wave_rows.shape[0]
    cond = wave_rows[:, NV:].astype(jnp.float32)
    cond_re = cond[:, :, 0]
    cond_im = cond[:, :, 1]
    out_re = jnp.einsum("kcg,kvg->kvc", cond_re, e_re) - jnp.einsum("kcg,kvg->kvc", cond_im, e_im)
    out_im = jnp.einsum("kcg,kvg->kvc", cond_re, e_im) + jnp.einsum("kcg,kvg->kvc", cond_im, e_re)
    return jnp.stack([out_re, out_im], axis=1).reshape(count, -1)


def any_blocks(wavefunc, haydock, screened, coulomb, umklapp_map):
    row_count = wavefunc.shape[0]
    plane_count = wavefunc.shape[3]
    share = row_count // lax.axis_size("pair")
    member = lax.axis_index("pair")
    amplitude = make_amplitude(wavefunc, haydock)
    partner = jnp.concatenate([amplitude, wavefunc[:, NV:]], axis=1)
    current = lax.dynamic_slice_in_dim(partner, member * share, share, 0)
    full_re, full_im = densities(wavefunc)
    share_re = lax.dynamic_slice_in_dim(full_re, member * share, share, 0)
    share_im = lax.dynamic_slice_in_dim(full_im, member * share, share, 0)
    hay_share = lax.dynamic_slice_in_dim(haydock, member * share, share, 0)
    x_re, x_im = fold_exchange(share_re, share_im, hay_share)
    x_re, x_im = lax.psum((x_re, x_im), ("blk", "pair"))
    total_k = row_count * lax.axis_size("blk")
    exchange = exchange_terms(full_re, full_im, x_re, x_im, coulomb) * (
        1.0 / (8.0 * math.sqrt(plane_count * total_k))
    )
    scale_direct = -1.0 / (8.0 * math.sqrt(plane_count * row_count * (STOPS + 1)))
    e_re = jnp.zeros((row_count, NV, plane_count), jnp.float32)
    e_im = jnp.zeros((row_count, NV, plane_count), jnp.float32)
    for stop_index in range(STOPS + 1):
        if stop_index > 0:
            current = from_behind(current, "blk", 1)
        weight = from_root(screened[0], "blk", stop_index)
        permuted = jnp.take(current, umklapp_map[stop_index], axis=3)
        d_re, d_im = direct_fold(wavefunc, permuted, weight)
        e_re = e_re + d_re
        e_im = e_im + d_im
    direct = finish_direct(wavefunc, e_re, e_im) * scale_direct
    return lax.psum(direct, "pair") + exchange


def solution(mesh):
    placed = (
        P(("grp", "blk"), None, None, None),
        P(("grp", "blk"), None),
        P(("grp", "blk"), None, None),
        P("grp"),
        P(),
    )
    body = eight_blocks if mesh.shape["blk"] == BLOCKS and mesh.shape["pair"] == 2 else any_blocks
    return jax.shard_map(body, mesh=mesh, in_specs=placed, out_specs=P(("grp", "blk"), None), check_vma=False)
```

profile of v0, /device:TPU:0, one launch (start us, length us, event | category | flops | bytes accessed | tf_op | source)
XLA Modules:
  0.0 46.4 jit_solution(14228401141073924831)
XLA Ops:
  0.0 0.0 copy-start
  0.0 0.0 copy-start.1
  0.0 1.2 %reshape.6.flat = bf16[192,768]{1,0:T(8,128)(2,1)S(1)} reshape(bf16[6,16,2,768]{3,2,1,0:T(2,128)(2,1)} %param.5) | data formatting | bytes 589824 | tf_op jit(solution)/shard_map/reshape | solution.py:359
  1.2 0.0 copy-start.2
  1.2 0.7 %copy-done.2 = f32[6,128]{1,0:T(8,128)S(1)} copy-done((f32[6,128]{1,0:T(8,128)S(1)}, f32[6,128]{1,0:T(8,128)}, u32[]{:S(2)}) %copy-start.2) | copy-done | bytes 3096
  1.9 4.8 %collective-permute-start = (bf16[208,768]{1,0:T(8,128)(2,1)S(1)}, bf16[208,768]{1,0:T(8,128)(2,1)S(1)}, u32[]{:S(2)}, u32[]{:S(2)}) collective-permute-start(bf16[208,768]{1,0:T(8,128)(2,1)S(1)} %shard_map.56.refs_0_), channel_id=1, source_target_pairs={{2,0},{5,1},{0,2},{7,3},{13,5},{15,7},{10,8},{12,9},{8,10},{14,11}... | collective-permute-start | bytes 958472 | tf_op jit(solution)/shard_map/ppermute | solution.py:340
  6.8 0.1 pad_add_fusion.who
  6.8 0.0 copy-done
  6.8 0.0 copy-done.1
  6.8 0.8 %shard_map.55 = (bf16[768,768]{1,0:T(8,128)(2,1)S(1)}, bf16[384,768]{1,0:T(8,128)(2,1)S(1)}) custom-call(s32[2]{0:T(128)S(1)} %pad_add_fusion.who, s32[3,768]{1,0:T(4,128)S(1)} %copy-done.1, bf16[768,768]{1,0:T(8,128)(2,1)S(1)} %bitcast.3), custom_call_target="tpu_custom_call" | custom-call | bytes 2958344 | tf_op jit(solution)/shard_map/pallas_call | solution.py:320
  7.6 4.5 %collective-permute-start.2 = (bf16[384,768]{1,0:T(8,128)(2,1)S(1)}, bf16[384,768]{1,0:T(8,128)(2,1)S(1)}, u32[]{:S(2)}, u32[]{:S(2)}) collective-permute-start(bf16[384,768]{1,0:T(8,128)(2,1)S(1)} %get-tuple-element.54), channel_id=1, source_target_pairs={{0,8},{2,10},{4,6},{1,9},{3,11},{5,7},{16,24},{18,26},{20,22},{17,... | collective-permute-start | bytes 1769480 | tf_op jit(solution)/shard_map/ppermute | solution.py:363
  12.2 1.8 %shard_map.57 = (bf16[1,192,768]{2,1,0:T(8,128)(2,1)S(1)}, bf16[1,768,96]{2,1,0:T(8,128)(2,1)S(1)}, bf16[1,96,768]{2,1,0:T(8,128)(2,1)S(1)}, bf16[96,768]{1,0:T(...) custom-call(s32[2]{0:T(128)S(1)} %pad_add_fusion.who, ...), custom_call_target="tpu_custom_call" | custom-call | bytes 2390024 | tf_op jit(solution)/shard_map/pallas_call | solution.py:320
  14.0 0.0 copy-start.3
  14.0 0.0 collective-permute-done.refs_0_
  14.0 0.1 collective-permute-start.3
  14.1 4.0 %collective-permute-start.1 = (bf16[208,768]{1,0:T(8,128)(2,1)S(1)}, bf16[208,768]{1,0:T(8,128)(2,1)S(1)}, u32[]{:S(2)}, u32[]{:S(2)}) collective-permute-start(bf16[208,768]{1,0:T(8,128)(2,1)S(1)} %shard_map.56.refs_0_), channel_id=1, source_target_pairs={{7,1},{14,2},{5,3},{0,4},{9,5},{2,6},{11,7},{15,9},{6,10},{13,11},... | collective-permute-start | bytes 958472 | tf_op jit(solution)/shard_map/ppermute | solution.py:340
  18.1 0.0 collective-permute-done.3.refs_1_
  18.1 2.5 %shard_map.58 = (bf16[2,192,768]{2,1,0:T(8,128)(2,1)S(1)}, bf16[2,768,96]{2,1,0:T(8,128)(2,1)S(1)}, bf16[2,96,768]{2,1,0:T(8,128)(2,1)S(1)}, bf16[192,768]{1,0:T...) custom-call(s32[2]{0:T(128)S(1)} %pad_add_fusion.who, ...), custom_call_target="tpu_custom_call" | custom-call | bytes 3594248 | tf_op jit(solution)/shard_map/pallas_call | solution.py:320
  20.6 2.0 %collective-permute-done.2.w_in = bf16[384,768]{1,0:T(8,128)(2,1)S(1)} collective-permute-done((bf16[384,768]{1,0:T(8,128)(2,1)S(1)}, bf16[384,768]{1,0:T(8,128)(2,1)S(1)}, u32[]{:S(2)}, u32[]{:S(2)}) %collective-permute-start.2) | collective-permute-done | bytes 589856 | tf_op jit(solution)/shard_map/ppermute | solution.py:363
  22.6 3.4 %collective-permute-done.1.msg = bf16[208,768]{1,0:T(8,128)(2,1)S(1)} collective-permute-done((bf16[208,768]{1,0:T(8,128)(2,1)S(1)}, bf16[208,768]{1,0:T(8,128)(2,1)S(1)}, u32[]{:S(2)}, u32[]{:S(2)}) %collective-permute-start.1) | collective-permute-done | bytes 319520 | tf_op jit(solution)/shard_map/ppermute | solution.py:340
  26.0 0.0 collective-permute-start.4
  26.0 1.3 %shard_map.59 = (bf16[96,768]{1,0:T(8,128)(2,1)S(1)}, bf16[96,768]{1,0:T(8,128)(2,1)S(1)}, bf16[96,768]{1,0:T(8,128)(2,1)S(1)}, f32[2,768]{1,0:T(2,128)S(1)}) custom-call(s32[2]{0:T(128)S(1)} %pad_add_fusion.who, bf16[208,768]{1,0:T(8,128)(2,1)S(1)} %collective-permute-done.1.msg, f32[2,768]{1,0:T(2,128)S(1)} %get-tuple-element.74.xs_0, ...), custom_call_target="tpu_custom_call" | custom-call | bytes 780296 | tf_op jit(solution)/shard_map/pallas_call | solution.py:320
  27.3 4.4 %collective-permute-start.6 = (f32[2,768]{1,0:T(2,128)S(1)}, f32[2,768]{1,0:T(2,128)S(1)}, u32[]{:S(2)}, u32[]{:S(2)}) collective-permute-start(f32[2,768]{1,0:T(2,128)S(1)} %get-tuple-element.83.refs_0_), channel_id=1, source_target_pairs={{0,8},{8,0},{1,9},{9,1},{16,24},{24,16},{17,25},{25,17}} | collective-permute-start | bytes 18440 | tf_op jit(solution)/shard_map/ppermute | solution.py:375
  31.7 0.1 collective-permute-start.5
  31.8 1.9 %collective-permute-done.6.refs_2_ = f32[2,768]{1,0:T(2,128)S(1)} collective-permute-done((f32[2,768]{1,0:T(2,128)S(1)}, f32[2,768]{1,0:T(2,128)S(1)}, u32[]{:S(2)}, u32[]{:S(2)}) %collective-permute-start.6) | collective-permute-done | bytes 6176 | tf_op jit(solution)/shard_map/ppermute | solution.py:375
  33.7 0.0 collective-permute-start.7
  33.7 0.0 copy-done.3
  33.7 0.0 collective-permute-done.4.w_swapped
  33.7 4.3 %shard_map.60 = (f32[2,96,96]{2,1,0:T(8,128)S(1)}, bf16[2,96,768]{2,1,0:T(8,128)(2,1)S(1)}, bf16[2,96,768]{2,1,0:T(8,128)(2,1)S(1)}, bf16[2,96,768]{2,1,0:T(8,128)(2,1)S(1)}) custom-call(s32[2]{0:T(128)S(1)} %pad_add_fusion.who, bf16[768,768]{1,0:T(8,128)(2,1)S(1)} %get-tuple-element.46.perm, bf16[768,768]{1,0:T(8,128)(2,1)S(1)} %bitcast.4, ...), custom_call_target="tpu_custom_call" | custom-call | bytes 7593992 | tf_op jit(solution)/shard_map/pallas_call | solution.py:320
  38.0 0.0 collective-permute-done.5.refs_1_
  38.0 0.0 collective-permute-done.7.refs_3_
  38.0 1.1 %shard_map.61 = (f32[6,128]{1,0:T(8,128)S(1)}, f32[6,128]{1,0:T(8,128)S(1)}, f32[6,128]{1,0:T(8,128)S(1)}) custom-call(s32[2]{0:T(128)S(1)} %pad_add_fusion.who, f32[2,96,96]{2,1,0:T(8,128)S(1)} %get-tuple-element.79.d_ref, bf16[2,96,768]{2,1,0:T(8,128)(2,1)S(1)} %get-tuple-element.80.v, bf16[2,96,768]{2,1,0:T(8,128)(2,1)S(1)} %get-tuple-element.81.ca, ...), custom_call_target="tpu_custom_call" | custom-call | bytes 995336 | tf_op jit(solution)/shard_map/pallas_call | solution.py:320
  39.2 1.9 %collective-permute-start.8 = (f32[6,128]{1,0:T(8,128)S(1)}, f32[6,128]{1,0:T(8,128)S(1)}, u32[]{:S(2)}, u32[]{:S(2)}) collective-permute-start(f32[6,128]{1,0:T(8,128)S(1)} %get-tuple-element.85), channel_id=1, source_target_pairs={{0,2},{1,5},{2,0},{3,7},{4,1},{5,13},{6,3},{7,15},{8,10},{9,14},{1... | collective-permute-start | bytes 9224 | tf_op jit(solution)/shard_map/ppermute | solution.py:340
  41.1 0.7 %collective-permute-start.9 = (f32[6,128]{1,0:T(8,128)S(1)}, f32[6,128]{1,0:T(8,128)S(1)}, u32[]{:S(2)}, u32[]{:S(2)}) collective-permute-start(f32[6,128]{1,0:T(8,128)S(1)} %get-tuple-element.86), channel_id=1, source_target_pairs={{1,7},{3,5},{5,9},{7,11},{9,13},{11,15},{17,23},{19,21},{21,25},{2... | collective-permute-start | bytes 9224 | tf_op jit(solution)/shard_map/ppermute | solution.py:340
  41.8 2.9 %collective-permute-done.8 = f32[6,128]{1,0:T(8,128)S(1)} collective-permute-done((f32[6,128]{1,0:T(8,128)S(1)}, f32[6,128]{1,0:T(8,128)S(1)}, u32[]{:S(2)}, u32[]{:S(2)}) %collective-permute-start.8) | collective-permute-done | bytes 3104 | tf_op jit(solution)/shard_map/ppermute | solution.py:340
  44.7 0.0 collective-permute-done.9
  44.7 0.1 collective-permute-start.10
  44.8 1.1 %collective-permute-done.10 = f32[6,128]{1,0:T(8,128)S(1)} collective-permute-done((f32[6,128]{1,0:T(8,128)S(1)}, f32[6,128]{1,0:T(8,128)S(1)}, u32[]{:S(2)}, u32[]{:S(2)}) %collective-permute-start.10) | collective-permute-done | bytes 3104 | tf_op jit(solution)/shard_map/ppermute | solution.py:343
  45.8 0.6 %add.11 = f32[6,128]{1,0:T(8,128)} add(f32[6,128]{1,0:T(8,128)S(1)} %add_add_fusion, f32[6,128]{1,0:T(8,128)S(1)} %collective-permute-done.10) | non-fusion elementwise | flops 768 | bytes 9216 | tf_op jit(solution)/shard_map/add | solution.py:400
  (3 shorter events, 0.0 us)
Async XLA Ops:
  0.0 6.8 %copy-start = (bf16[1,768,768]{2,1,0:T(8,128)(2,1)S(1)}, bf16[1,768,768]{2,1,0:T(8,128)(2,1)}, u32[]{:S(2)}) copy-start(bf16[1,768,768]{2,1,0:T(8,128)(2,1)} %param.7) | copy-start | bytes 3538948
  0.0 6.8 %copy-start.1 = (s32[3,768]{1,0:T(4,128)S(1)}, s32[3,768]{1,0:T(4,128)}, u32[]{:S(2)}) copy-start(s32[3,768]{1,0:T(4,128)} %umk.1) | copy-start | bytes 27652
  1.2 0.7 %copy-start.2 = (f32[6,128]{1,0:T(8,128)S(1)}, f32[6,128]{1,0:T(8,128)}, u32[]{:S(2)}) copy-start(f32[6,128]{1,0:T(8,128)} %hay.1) | copy-start | bytes 9220
  1.9 12.1 %collective-permute-start = (bf16[208,768]{1,0:T(8,128)(2,1)S(1)}, bf16[208,768]{1,0:T(8,128)(2,1)S(1)}, u32[]{:S(2)}, u32[]{:S(2)}) collective-permute-start(bf16[208,768]{1,0:T(8,128)(2,1)S(1)} %shard_map.56.refs_0_), channel_id=1, source_target_pairs={{2,0},{5,1},{0,2},{7,3},{13,5},{15,7},{10,8},{12,9},{8,10},{14,11}... | collective-permute-start | bytes 958472 | tf_op jit(solution)/shard_map/ppermute | solution.py:340
  7.6 15.0 %collective-permute-start.2 = (bf16[384,768]{1,0:T(8,128)(2,1)S(1)}, bf16[384,768]{1,0:T(8,128)(2,1)S(1)}, u32[]{:S(2)}, u32[]{:S(2)}) collective-permute-start(bf16[384,768]{1,0:T(8,128)(2,1)S(1)} %get-tuple-element.54), channel_id=1, source_target_pairs={{0,8},{2,10},{4,6},{1,9},{3,11},{5,7},{16,24},{18,26},{20,22},{17,... | collective-permute-start | bytes 1769480 | tf_op jit(solution)/shard_map/ppermute | solution.py:363
  14.0 19.7 %copy-start.3 = (f32[768]{0:T(1024)S(1)}, f32[768]{0:T(1024)}, u32[]{:S(2)}) copy-start(f32[768]{0:T(1024)} %param.8) | copy-start | bytes 9220
  14.0 4.1 %collective-permute-start.3 = (bf16[208,768]{1,0:T(8,128)(2,1)S(1)}, bf16[208,768]{1,0:T(8,128)(2,1)S(1)}, u32[]{:S(2)}, u32[]{:S(2)}) collective-permute-start(bf16[208,768]{1,0:T(8,128)(2,1)S(1)} %collective-permute-done.refs_0_), channel_id=1, source_target_pairs={{0,1},{1,0},{2,3},{3,2},{4,5},{5,4},{6,7},{7,6},{8,9},{9,8},{10,11... | collective-permute-start | bytes 958472 | tf_op jit(solution)/shard_map/ppermute | solution.py:343
  14.1 11.9 %collective-permute-start.1 = (bf16[208,768]{1,0:T(8,128)(2,1)S(1)}, bf16[208,768]{1,0:T(8,128)(2,1)S(1)}, u32[]{:S(2)}, u32[]{:S(2)}) collective-permute-start(bf16[208,768]{1,0:T(8,128)(2,1)S(1)} %shard_map.56.refs_0_), channel_id=1, source_target_pairs={{7,1},{14,2},{5,3},{0,4},{9,5},{2,6},{11,7},{15,9},{6,10},{13,11},... | collective-permute-start | bytes 958472 | tf_op jit(solution)/shard_map/ppermute | solution.py:340
  26.0 7.7 %collective-permute-start.4 = (bf16[384,768]{1,0:T(8,128)(2,1)S(1)}, bf16[384,768]{1,0:T(8,128)(2,1)S(1)}, u32[]{:S(2)}, u32[]{:S(2)}) collective-permute-start(bf16[384,768]{1,0:T(8,128)(2,1)S(1)} %collective-permute-done.2.w_in), channel_id=1, source_target_pairs={{0,1},{1,0},{2,3},{3,2},{4,5},{5,4},{6,7},{7,6},{8,9},{9,8},{10,11... | collective-permute-start | bytes 1769480 | tf_op jit(solution)/shard_map/ppermute | solution.py:343
  27.3 6.4 %collective-permute-start.6 = (f32[2,768]{1,0:T(2,128)S(1)}, f32[2,768]{1,0:T(2,128)S(1)}, u32[]{:S(2)}, u32[]{:S(2)}) collective-permute-start(f32[2,768]{1,0:T(2,128)S(1)} %get-tuple-element.83.refs_0_), channel_id=1, source_target_pairs={{0,8},{8,0},{1,9},{9,1},{16,24},{24,16},{17,25},{25,17}} | collective-permute-start | bytes 18440 | tf_op jit(solution)/shard_map/ppermute | solution.py:375
  31.7 6.3 %collective-permute-start.5 = (f32[2,768]{1,0:T(2,128)S(1)}, f32[2,768]{1,0:T(2,128)S(1)}, u32[]{:S(2)}, u32[]{:S(2)}) collective-permute-start(f32[2,768]{1,0:T(2,128)S(1)} %get-tuple-element.83.refs_0_), channel_id=1, source_target_pairs={{0,1},{1,0},{2,3},{3,2},{4,5},{5,4},{6,7},{7,6},{8,9},{9,8},{10,11... | collective-permute-start | bytes 18440 | tf_op jit(solution)/shard_map/ppermute | solution.py:343
  33.7 4.3 %collective-permute-start.7 = (f32[2,768]{1,0:T(2,128)S(1)}, f32[2,768]{1,0:T(2,128)S(1)}, u32[]{:S(2)}, u32[]{:S(2)}) collective-permute-start(f32[2,768]{1,0:T(2,128)S(1)} %collective-permute-done.6.refs_2_), channel_id=1, source_target_pairs={{0,1},{1,0},{2,3},{3,2},{4,5},{5,4},{6,7},{7,6},{8,9},{9,8},{10,11... | collective-permute-start | bytes 18440 | tf_op jit(solution)/shard_map/ppermute | solution.py:343
  39.2 5.5 %collective-permute-start.8 = (f32[6,128]{1,0:T(8,128)S(1)}, f32[6,128]{1,0:T(8,128)S(1)}, u32[]{:S(2)}, u32[]{:S(2)}) collective-permute-start(f32[6,128]{1,0:T(8,128)S(1)} %get-tuple-element.85), channel_id=1, source_target_pairs={{0,2},{1,5},{2,0},{3,7},{4,1},{5,13},{6,3},{7,15},{8,10},{9,14},{1... | collective-permute-start | bytes 9224 | tf_op jit(solution)/shard_map/ppermute | solution.py:340
  41.1 3.6 %collective-permute-start.9 = (f32[6,128]{1,0:T(8,128)S(1)}, f32[6,128]{1,0:T(8,128)S(1)}, u32[]{:S(2)}, u32[]{:S(2)}) collective-permute-start(f32[6,128]{1,0:T(8,128)S(1)} %get-tuple-element.86), channel_id=1, source_target_pairs={{1,7},{3,5},{5,9},{7,11},{9,13},{11,15},{17,23},{19,21},{21,25},{2... | collective-permute-start | bytes 9224 | tf_op jit(solution)/shard_map/ppermute | solution.py:340
  44.7 1.2 %collective-permute-start.10 = (f32[6,128]{1,0:T(8,128)S(1)}, f32[6,128]{1,0:T(8,128)S(1)}, u32[]{:S(2)}, u32[]{:S(2)}) collective-permute-start(f32[6,128]{1,0:T(8,128)S(1)} %add_add_fusion), channel_id=1, source_target_pairs={{0,1},{1,0},{2,3},{3,2},{4,5},{5,4},{6,7},{7,6},{8,9},{9,8},{10,11... | collective-permute-start | bytes 9224 | tf_op jit(solution)/shard_map/ppermute | solution.py:343
where the time goes:
time: 46.7 us; the launch traced here: 46.4 us
  starting transfers between devices  20.6 us (44%)
  Pallas kernels  11.8 us (25%)
  waiting for transfers between devices  11.3 us (24%)
  local copies, waits for them, and re-layouts  1.87 us (4%)
  other arithmetic  0.67 us (1%)
    pallas_call x7, Pallas kernels, call(): pl.pallas_call(kernel, out_shape=outs, in_specs=specs, out_specs=[VM] * l...  11.8 us
    ppermute x4, starting transfers between devices, over_cores(): return lax.ppermute(x, ('blk', 'pair'), pairs)  11.4 us
    ppermute x4, waiting for transfers between devices, over_cores(): return lax.ppermute(x, ('blk', 'pair'), pairs)  6.33 us
    ppermute x1, starting transfers between devices, eight_blocks(): w_in = lax.ppermute(w_half, 'blk', MATRIX_MOVES)  4.53 us
    ppermute x1, starting transfers between devices, eight_blocks(): xs_in = lax.ppermute(xs, 'blk', SUMS)  4.44 us
    ppermute x1, waiting for transfers between devices, eight_blocks(): w_in = lax.ppermute(w_half, 'blk', MATRIX_MOVES)  2 us
    ppermute x1, waiting for transfers between devices, eight_blocks(): xs_in = lax.ppermute(xs, 'blk', SUMS)  1.89 us
    reshape x1, local copies, waits for them, and re-layouts, eight_blocks(): flat = wavefunc.reshape(kr * nb * 2, planes)  1.17 us
  transfers between devices with their start and end apart: 11, of which 5 were waited for; matrix products, arithmetic and copies ran while one was open for 0% of the time, Pallas kernels for 23%

commit v1 on v0

--- a/solution.py
+++ b/solution.py
@@ -26,12 +26,12 @@
 }
 MATRIX_MOVES = ((0, 4), (1, 5), (2, 3))
 FETCH = {
-    (0, 0): (1, None), (0, 1): (2, 3),
-    (1, 0): (0, 7), (1, 1): (3, 2),
-    (2, 0): (None, 0), (2, 1): (6, 4),
-    (3, 0): (None, 1), (3, 1): (7, 5),
-    (4, 0): (5, None), (4, 1): (6, 7),
-    (5, 0): (4, 3), (5, 1): (7, 6),
+    (0, 0): (3, 2), (0, 1): (1, 2),
+    (1, 0): (0, 7), (1, 1): (2, 3),
+    (2, 0): (0, None), (2, 1): (6, 4),
+    (3, 0): (1, None), (3, 1): (7, 5),
+    (4, 0): (5, 6), (4, 1): (7, 6),
+    (5, 0): (3, 4), (5, 1): (6, 7),
 }
 SUMS = ((0, 4), (4, 0))
 
@@ -93,7 +93,7 @@
     return lax.dot_general(a, b, (dims, ((), ())), preferred_element_type=F32, **kw)
 
 
-def message_kernel(flat, hay, mine):
+def message_kernel(flat, hay, mine, again):
     rows, planes = flat.shape
     kr = hay.shape[0]
     mine[0:rows, :] = flat[...]
@@ -103,12 +103,12 @@
     both = jnp.concatenate([hi.astype(F32), lo.astype(F32)], axis=1)
     mine[rows : rows + 16, :] = jnp.zeros((16, planes), BF)
     mine[rows : rows + 16, 0:256] = jnp.concatenate([both, jnp.zeros((16 - kr, 256), F32)], axis=0).astype(BF)
-
-
-def perm_kernel(who, umk, screened, perm, w_half):
+    again[0 : rows + 16, :] = mine[...]
+    again[rows + 16 :, :] = jnp.zeros((again.shape[0] - rows - 16, planes), BF)
+
+
+def perm_kernel(who, umk, perm):
     planes = perm.shape[0]
-    gh = w_half.shape[0]
-    w_half[...] = screened[pl.ds(pl.multiple_of(who[1] * gh, 128), gh), :]
     row = umk[pl.ds(entry(who, 1), 1), :]
     perm[...] = one(iota((planes, planes), 0) == row).astype(BF)
 
@@ -165,54 +165,41 @@
         cb_refs[j][...] = (-dot(turn, c[part, :])).astype(BF)
 
 
-def prep_kernel(n, who, perm, *refs):
-    msgs, (ap, wt, v, ca, cb, xs, a_scr) = refs[:n], refs[n:]
+def prep_kernel(n, n_sums, who, perm, *refs):
+    msgs, earlier, (ap, wt, v, ca, cb, xs, a_scr) = refs[:n], refs[n : n + n_sums], refs[n + n_sums :]
     rows, planes = v.shape[1:]
+    total = jnp.zeros((2, planes), F32)
+    for ref in earlier:
+        total = total + ref[...]
+    for j in range(n):
+        mine = pl.ds(j * rows, rows)
+        amp, turned = amplitude(msgs[j], v.at[j], ca.at[mine])
+        total = total + sums(ca.at[mine], amp, turned)
+        a_scr[mine, :] = amp.astype(BF)
+    xs[...] = total
 
     @pl.when(entry(who, 0) == 1)
     def _():
-        total = jnp.zeros((2, planes), F32)
-        for j in range(n):
-            mine = pl.ds(j * rows, rows)
-            amp, turned = amplitude(msgs[j], v.at[j], ca.at[mine])
-            total = total + sums(ca.at[mine], amp, turned)
-            a_scr[mine, :] = amp.astype(BF)
-        xs[...] = total
         each = range(n)
         permute(a_scr, ca, perm, [ap.at[j] for j in each], [wt.at[j] for j in each], [cb.at[j] for j in each])
 
-    @pl.when(entry(who, 0) == 0)
-    def _():
-        xs[...] = jnp.zeros_like(xs)
-
-
-def last_kernel(who, msg, xs_0, xs_1, v, c, a, xs):
+
+def last_kernel(who, msg, earlier, v, c, a, xs):
     @pl.when(entry(who, 0) == 1)
     def _():
         amp, turned = amplitude(msg, v, c)
         a[...] = amp.astype(BF)
-        xs[...] = xs_0[...] + xs_1[...] + sums(c, amp, turned)
+        xs[...] = earlier[...] + sums(c, amp, turned)
 
     @pl.when(entry(who, 0) == 0)
     def _():
         xs[...] = jnp.zeros_like(xs)
 
 
-def main_kernel(who, perm, w_own, w_in, w_swapped, *refs):
+def pick_kernel(who, perm, *refs):
     own, two, (v_3, c_3, a_3) = refs[0:5], refs[5:10], refs[10:13]
-    d_ref, vt_ref, ca_ref, cb_ref, wf, ap_3, wt_3, cb_3, ap_scr, wt_scr = refs[13:]
-    rows, planes = v_3.shape
-    gh = planes // 2
-    p = who[1]
-
-    @pl.when((entry(who, 0) == 1) & (entry(who, 2) == 0))
-    def _():
-        wf[...] = w_own[...].astype(F32)
-
-    @pl.when((entry(who, 0) == 1) & (entry(who, 2) == 1))
-    def _():
-        wf[pl.ds(pl.multiple_of(p * gh, 128), gh), :] = w_in[...].astype(F32)
-        wf[pl.ds(pl.multiple_of((1 - p) * gh, 128), gh), :] = w_swapped[...].astype(F32)
+    ap_ref, wt_ref, vt_ref, ca_ref, cb_ref, ap_3, wt_3, cb_3 = refs[13:]
+    rows = v_3.shape[0]
 
     @pl.when(entry(who, 0) == 1)
     def _():
@@ -236,7 +223,22 @@
             @pl.when((entry(who, 0) == 1) & (entry(who, 6 + i) == slot))
             def _(i=i, slot=slot):
                 ap, wt = held(slot)[:2]
-                ap_scr[i], wt_scr[i] = ap[...], wt[...]
+                ap_ref[i], wt_ref[i] = ap[...], wt[...]
+
+
+def main_kernel(who, w_own, w_in, w_swapped, ap, wt, v, ca, cb, d_ref, wf):
+    rows, planes = v.shape[1:]
+    gh = planes // 2
+    p = who[1]
+
+    @pl.when((entry(who, 0) == 1) & (entry(who, 2) == 0))
+    def _():
+        wf[...] = w_own[...].astype(F32)
+
+    @pl.when((entry(who, 0) == 1) & (entry(who, 2) == 1))
+    def _():
+        wf[pl.ds(pl.multiple_of(p * gh, 128), gh), :] = w_in[...].astype(F32)
+        wf[pl.ds(pl.multiple_of((1 - p) * gh, 128), gh), :] = w_swapped[...].astype(F32)
 
     @pl.when(entry(who, 0) == 1)
     def _():
@@ -244,9 +246,9 @@
         for i in range(2):
             for h in range(2):
                 w = wf[h * gh : (h + 1) * gh, :]
-                left = wt_scr[i, h * gh : (h + 1) * gh, :]
-                k_re = (w * dot(left, ap_scr[i, 0:rows, :])).astype(BF)
-                k_im = (w * dot(left, ap_scr[i, rows : 2 * rows, :])).astype(BF)
+                left = wt[i, h * gh : (h + 1) * gh, :]
+                k_re = (w * dot(left, ap[i, 0:rows, :])).astype(BF)
+                k_im = (w * dot(left, ap[i, rows : 2 * rows, :])).astype(BF)
                 kernels.append((k_re, k_im))
         sides = []
         for i in range(2):
@@ -254,15 +256,15 @@
             for h in range(2):
                 k_re, k_im = kernels[2 * i + h]
                 part = slice(h * gh, (h + 1) * gh)
-                z = dot(ca_ref[i, :, part], k_re) + dot(cb_ref[i, :, part], k_im)
+                z = dot(ca[i, :, part], k_re) + dot(cb[i, :, part], k_im)
                 y = z if y is None else y + z
             sides.append(y.astype(BF))
         for i, y in enumerate(sides):
-            d_ref[i] = dot(y, vt_ref[i], ((1,), (1,)))
+            d_ref[i] = dot(y, v[i], ((1,), (1,)))
 
 
 def finish_kernel(scale_direct, scale_exchange, who, d_ref, v, ca, cb, *refs):
-    xs, xs_swapped, xs_in, xs_in_swapped, coulomb, stays, goes_1, goes_2 = refs
+    xs, xs_in, coulomb, stays, goes_1, goes_2 = refs
     rows = v.shape[1]
     kr = rows // 16
     p = who[1]
@@ -301,8 +303,7 @@
 
     @pl.when((entry(who, 0) == 1) & (entry(who, 3) == 1))
     def _():
-        total = jnp.where(p == 1, xs[...] + xs_in[...], xs_swapped[...] + xs_in_swapped[...])
-        y = coulomb[...] * total * scale_exchange
+        y = coulomb[...] * (xs[...] + xs_in[...]) * scale_exchange
         both = []
         for i in range(2):
             side = (ca[i].astype(F32) * y[0:1] + cb[i].astype(F32) * y[1:2]).astype(BF)
@@ -314,9 +315,12 @@
 SM = pl.BlockSpec(memory_space=pltpu.SMEM)
 
 
-def call(kernel, outs, ins, scratch=(), limit=24 << 20):
-    moved = sum(math.prod(x.shape) * x.dtype.itemsize for x in (*ins, *outs))
+def call(kernel, outs, ins, scratch=(), known=True, limit=24 << 20):
+    moved = sum(math.prod(x.shape) * x.dtype.itemsize for x in (*ins, *outs)) if known else 0
     specs = [SM if x.dtype == jnp.int32 and x.ndim == 1 else VM for x in ins]
+    if not known:
+        ins = [x if x.dtype == jnp.int32 else pltpu.with_memory_space_constraint(x, pltpu.VMEM) for x in ins]
+        outs = [pltpu.VMEM(x.shape, x.dtype) for x in outs]
     return pl.pallas_call(
         kernel,
         out_shape=outs,
@@ -328,6 +332,9 @@
     )(*ins)
 
 
+PAD = 16
+
+
 def eight_blocks(wavefunc, haydock, screened, coulomb, umklapp_map):
     kr, nb, _, planes = wavefunc.shape
     rows = kr * 16
@@ -342,7 +349,7 @@
     def swap(x):
         return lax.ppermute(x, "pair", [(0, 1), (1, 0)])
 
-    def prep(perm, msgs):
+    def prep(perm, msgs, earlier=(), known=True):
         n = len(msgs)
         outs = [
             shape((n, 2 * rows, planes), BF),
@@ -353,48 +360,52 @@
             shape((2, planes), F32),
         ]
         return call(
-            functools.partial(prep_kernel, n), outs, [who, perm, *msgs], scratch=[pltpu.VMEM((n * rows, planes), BF)]
+            functools.partial(prep_kernel, n, len(earlier)),
+            outs,
+            [who, perm, *msgs, *earlier],
+            scratch=[pltpu.VMEM((n * rows, planes), BF)],
+            known=known,
         )
 
+    w_in = lax.ppermute(lax.dynamic_slice_in_dim(screened[0], member * gh, gh, 0), "blk", MATRIX_MOVES)
     flat = wavefunc.reshape(kr * nb * 2, planes)
-    perm, w_half = call(
-        perm_kernel, [shape((planes, planes), BF), shape((gh, planes), BF)], [who, umklapp_map, screened[0]]
-    )
-    w_in = lax.ppermute(w_half, "blk", MATRIX_MOVES)
-    (mine,) = call(message_kernel, [shape((2 * rows + 16, planes), BF)], [flat, haydock])
+    sizes = (2 * rows + 16, 2 * rows + 16 + PAD)
+    mine, again = call(message_kernel, [shape((n, planes), BF) for n in sizes], [flat, haydock])
     got_1 = over_cores(mine, FETCH_ROUNDS[0])
+    (perm,) = call(perm_kernel, [shape((planes, planes), BF)], [who, umklapp_map])
     own = prep(perm, [mine])
-    got_1, mine, *own = lax.optimization_barrier((got_1, mine, *own))
-    got_2 = over_cores(mine, FETCH_ROUNDS[1])
-    two = prep(perm, [got_1, swap(got_1)])
-    got_2, w_in, *two = lax.optimization_barrier((got_2, w_in, *two))
+    got_1, *own = lax.optimization_barrier((got_1, *own))
+    got_2 = over_cores(again, FETCH_ROUNDS[1])
+    two = prep(perm, [got_1, swap(got_1)], [own[5]], known=False)
+    got_2, *two = lax.optimization_barrier((got_2, *two))
     bands = shape((rows, planes), BF)
-    v_3, c_3, a_3, xs = call(
-        last_kernel, [bands, bands, bands, shape((2, planes), F32)], [who, got_2, own[5], two[5]]
-    )
+    v_3, c_3, a_3, xs = call(last_kernel, [bands, bands, bands, shape((2, planes), F32)], [who, got_2, two[5]])
     xs_in = lax.ppermute(xs, "blk", SUMS)
-    xs_all = [xs, swap(xs), xs_in, swap(xs_in)]
     total_k = kr * lax.axis_size("blk")
     scale_exchange = 1.0 / (8.0 * math.sqrt(planes * total_k))
     scale_direct = -1.0 / (8.0 * math.sqrt(planes * kr * (STOPS + 1)))
     item = shape((2, rows, planes), BF)
-    d, v, ca, cb = call(
-        main_kernel,
-        [shape((2, rows, rows), F32), item, item, item],
-        [who, perm, screened[0], w_in, swap(w_in), *own[:5], *two[:5], v_3, c_3, a_3],
+    ap, wt, v, ca, cb = call(
+        pick_kernel,
+        [shape((2, 2 * rows, planes), BF), shape((2, planes, rows), BF), item, item, item],
+        [who, perm, *own[:5], *two[:5], v_3, c_3, a_3],
         scratch=[
-            pltpu.VMEM((planes, planes), F32),
             pltpu.VMEM((2 * rows, planes), BF),
             pltpu.VMEM((planes, rows), BF),
             pltpu.VMEM((rows, planes), BF),
-            pltpu.VMEM((2, 2 * rows, planes), BF),
-            pltpu.VMEM((2, planes, rows), BF),
         ],
+    )
+    w_in, ap, wt = lax.optimization_barrier((w_in, ap, wt))
+    (d,) = call(
+        main_kernel,
+        [shape((2, rows, rows), F32)],
+        [who, screened[0], w_in, swap(w_in), ap, wt, v, ca, cb],
+        scratch=[pltpu.VMEM((planes, planes), F32)],
     )
     stays, goes_1, goes_2 = call(
         functools.partial(finish_kernel, scale_direct, scale_exchange),
         [shape((kr, 128), F32)] * 3,
-        [who, d, v, ca, cb, *xs_all, coulomb.reshape(1, planes)],
+        [who, d, v, ca, cb, xs, xs_in, coulomb.reshape(1, planes)],
     )
     total = stays + over_cores(goes_1, HOME_ROUNDS[0]) + over_cores(goes_2, HOME_ROUNDS[1])
     return total + swap(total)

time: 46.7 us -> 41.3 us (0.88)
  starting transfers between devices: 20.6 us -> 15.4 us
  waiting for transfers between devices: 11.3 us -> 9.06 us
  local copies, waits for them, and re-layouts: 1.87 us -> 2.9 us
  Pallas kernels: 11.8 us -> 12.7 us
    ppermute x1, starting transfers between devices: 4.53 us -> 2.42 us  [eight_blocks(): lax.ppermute(lax.dynamic_slice_in_dim(screened[0], member * gh, gh, 0), '...]
    ppermute x1, waiting for transfers between devices: 2 us -> 0.01 us  [eight_blocks(): lax.ppermute(lax.dynamic_slice_in_dim(screened[0], member * gh, gh, 0), '...]
    ppermute x4, starting transfers between devices: 11.4 us -> 9.47 us  [over_cores(): return lax.ppermute(x, ('blk', 'pair'), pairs)]
    ppermute x1, waiting for transfers between devices: 1.89 us -> 0.01 us  [eight_blocks(): xs_in = lax.ppermute(xs, 'blk', SUMS)]
    ppermute x5 -> x3, waiting for transfers between devices: 1.06 us -> 2.77 us  [swap(): return lax.ppermute(x, 'pair', [(0, 1), (1, 0)])]
    dynamic_slice x0 -> x1, local copies, waits for them, and re-layouts: none -> 1.11 us  [eight_blocks(): lax.dynamic_slice_in_dim(screened[0], member * gh, gh, 0)]
    ppermute x1, starting transfers between devices: 4.44 us -> 3.34 us  [eight_blocks(): xs_in = lax.ppermute(xs, 'blk', SUMS)]
    pallas_call x7 -> x8, Pallas kernels: 11.8 us -> 12.7 us  [call(): pl.pallas_call(kernel, out_shape=outs, in_specs=specs, out_specs=[VM] * l...]
  transfers between devices with their start and end apart: 11 -> 9, of which waited for: 5 -> 4; matrix products, arithmetic and copies ran while one was open for 0% -> 3% of each run, Pallas kernels for 23% -> 28%
where the time goes in v1:
time: 41.3 us; the launch traced here: 40.9 us
  starting transfers between devices  15.4 us (37%)
  Pallas kernels  12.7 us (31%)
  waiting for transfers between devices  9.06 us (22%)
  local copies, waits for them, and re-layouts  2.9 us (7%)
  other arithmetic  0.67 us (2%)
    pallas_call x8, Pallas kernels, call(): pl.pallas_call(kernel, out_shape=outs, in_specs=specs, out_specs=[VM] * l...  12.7 us
    ppermute x4, starting transfers between devices, over_cores(): return lax.ppermute(x, ('blk', 'pair'), pairs)  9.47 us
    ppermute x4, waiting for transfers between devices, over_cores(): return lax.ppermute(x, ('blk', 'pair'), pairs)  6.29 us
    ppermute x1, starting transfers between devices, eight_blocks(): xs_in = lax.ppermute(xs, 'blk', SUMS)  3.34 us
    ppermute x3, waiting for transfers between devices, swap(): return lax.ppermute(x, 'pair', [(0, 1), (1, 0)])  2.77 us
    ppermute x1, starting transfers between devices, eight_blocks(): lax.ppermute(lax.dynamic_slice_in_dim(screened[0], member * gh, gh, 0), '...  2.42 us
    dynamic_slice x1, local copies, waits for them, and re-layouts, eight_blocks(): lax.dynamic_slice_in_dim(screened[0], member * gh, gh, 0)  1.11 us
    reshape x1, local copies, waits for them, and re-layouts, eight_blocks(): flat = wavefunc.reshape(kr * nb * 2, planes)  1.09 us
  transfers between devices with their start and end apart: 9, of which 4 were waited for; matrix products, arithmetic and copies ran while one was open for 3% of the time, Pallas kernels for 28%

profile of v1, /device:TPU:0, one launch (start us, length us, event | category | flops | bytes accessed | tf_op | source)
XLA Modules:
  0.0 40.9 jit_solution(14619081495148291506)
XLA Ops:
  0.0 0.0 copy-start.1
  0.0 1.1 %reshape.7.flat = bf16[192,768]{1,0:T(8,128)(2,1)S(1)} reshape(bf16[6,16,2,768]{3,2,1,0:T(2,128)(2,1)} %param.5) | data formatting | bytes 589824 | tf_op jit(solution)/shard_map/reshape | solution.py:371
  1.1 0.0 copy-start.2
  1.1 0.7 %copy-done.2 = f32[6,128]{1,0:T(8,128)S(1)} copy-done((f32[6,128]{1,0:T(8,128)S(1)}, f32[6,128]{1,0:T(8,128)}, u32[]{:S(2)}) %copy-start.2) | copy-done | bytes 3096
  1.8 4.8 %collective-permute-start.1 = (bf16[208,768]{1,0:T(8,128)(2,1)S(1)}, bf16[208,768]{1,0:T(8,128)(2,1)S(1)}, u32[]{:S(2)}, u32[]{:S(2)}) collective-permute-start(bf16[208,768]{1,0:T(8,128)(2,1)S(1)} %get-tuple-element.48.refs_0_), channel_id=1, source_target_pairs={{6,0},{3,1},{0,2},{5,3},{1,4},{13,5},{2,6},{15,7},{10,8},{14,9},{7... | collective-permute-start | bytes 958472 | tf_op jit(solution)/shard_map/ppermute | solution.py:347
  6.7 1.1 %dynamic-slice_bitcast_fusion = bf16[384,768]{1,0:T(8,128)(2,1)S(1)} fusion(bf16[1,768,768]{2,1,0:T(8,128)(2,1)} %param.7, s32[]{:T(128)S(6)} %select_n.3), kind=kLoop, calls=%fused_computation | loop fusion | bytes 1179652 | tf_op jit(solution)/shard_map/dynamic_slice | solution.py:370
  7.8 2.4 %collective-permute-start = (bf16[384,768]{1,0:T(8,128)(2,1)S(1)}, bf16[384,768]{1,0:T(8,128)(2,1)S(1)}, u32[]{:S(2)}, u32[]{:S(2)}) collective-permute-start(bf16[384,768]{1,0:T(8,128)(2,1)S(1)} %dynamic-slice_bitcast_fusion), channel_id=1, source_target_pairs={{0,8},{2,10},{4,6},{1,9},{3,11},{5,7},{16,24},{18,26},{20,22},{17,... | collective-permute-start | bytes 1769480 | tf_op jit(solution)/shard_map/ppermute | solution.py:370
  10.2 1.3 %collective-permute-start.2 = (bf16[224,768]{1,0:T(8,128)(2,1)S(1)}, bf16[224,768]{1,0:T(8,128)(2,1)S(1)}, u32[]{:S(2)}, u32[]{:S(2)}) collective-permute-start(bf16[224,768]{1,0:T(8,128)(2,1)S(1)} %get-tuple-element.60), channel_id=1, source_target_pairs={{4,0},{5,1},{14,2},{7,3},{9,5},{11,7},{12,8},{13,9},{8,10},{15,11}... | collective-permute-start | bytes 1032200 | tf_op jit(solution)/shard_map/ppermute | solution.py:347
  11.5 0.1 pad_add_fusion.who
  11.6 0.0 copy-done.1
  11.6 0.8 %shard_map.55.perm = bf16[768,768]{1,0:T(8,128)(2,1)S(1)} custom-call(s32[2]{0:T(128)S(1)} %pad_add_fusion.who, s32[3,768]{1,0:T(4,128)S(1)} %copy-done.1), custom_call_target="tpu_custom_call" | custom-call | bytes 1188872 | tf_op jit(solution)/shard_map/pallas_call | solution.py:324
  12.4 2.0 %shard_map.57 = (bf16[1,192,768]{2,1,0:T(8,128)(2,1)S(1)}, bf16[1,768,96]{2,1,0:T(8,128)(2,1)S(1)}, bf16[1,96,768]{2,1,0:T(8,128)(2,1)S(1)}, bf16[96,768]{1,0:T(...) custom-call(s32[2]{0:T(128)S(1)} %pad_add_fusion.who, bf16[768,768]{1,0:T(8,128)(2,1)S(1)} %shard_map.55.perm, ...), custom_call_target="tpu_custom_call" | custom-call | bytes 2390024 | tf_op jit(solution)/shard_map/pallas_call | solution.py:324
  14.4 0.0 collective-permute-done.1.refs_0_
  14.4 0.1 collective-permute-start.3
  14.4 1.6 %collective-permute-done.3.refs_1_ = bf16[208,768]{1,0:T(8,128)(2,1)S(1)} collective-permute-done((bf16[208,768]{1,0:T(8,128)(2,1)S(1)}, bf16[208,768]{1,0:T(8,128)(2,1)S(1)}, u32[]{:S(2)}, u32[]{:S(2)}) %collective-permute-start.3) | collective-permute-done | bytes 319520 | tf_op jit(solution)/shard_map/ppermute | solution.py:350
  16.0 2.7 %shard_map.58 = (bf16[2,192,768]{2,1,0:T(8,128)(2,1)S(1)}, bf16[2,768,96]{2,1,0:T(8,128)(2,1)S(1)}, bf16[2,96,768]{2,1,0:T(8,128)(2,1)S(1)}, bf16[192,768]{1,0:T...) custom-call(s32[2]{0:T(128)S(1)} %pad_add_fusion.who, bf16[768,768]{1,0:T(8,128)(2,1)S(1)} %shard_map.55.perm, ...), custom_call_target="tpu_custom_call" | custom-call | tf_op jit(solution)/shard_map/pallas_call | solution.py:324
  18.7 4.1 %collective-permute-done.2.msg = bf16[224,768]{1,0:T(8,128)(2,1)S(1)} collective-permute-done((bf16[224,768]{1,0:T(8,128)(2,1)S(1)}, bf16[224,768]{1,0:T(8,128)(2,1)S(1)}, u32[]{:S(2)}, u32[]{:S(2)}) %collective-permute-start.2) | collective-permute-done | bytes 344096 | tf_op jit(solution)/shard_map/ppermute | solution.py:347
  22.9 1.3 %shard_map.59 = (bf16[96,768]{1,0:T(8,128)(2,1)S(1)}, bf16[96,768]{1,0:T(8,128)(2,1)S(1)}, bf16[96,768]{1,0:T(8,128)(2,1)S(1)}, f32[2,768]{1,0:T(2,128)S(1)}) custom-call(s32[2]{0:T(128)S(1)} %pad_add_fusion.who, bf16[224,768]{1,0:T(8,128)(2,1)S(1)} %collective-permute-done.2.msg, f32[2,768]{1,0:T(2,128)S(1)} %get-tuple-element.75.earlier), custom_call_target="tpu_custom_call" | custom-call | bytes 798728 | tf_op jit(solution)/shard_map/pallas_call | solution.py:324
  24.1 0.0 copy-start.3
  24.1 0.0 copy-start
  24.2 1.7 %shard_map.60 = (bf16[2,192,768]{2,1,0:T(8,128)(2,1)S(1)}, bf16[2,768,96]{2,1,0:T(8,128)(2,1)S(1)}, bf16[2,96,768]{2,1,0:T(8,128)(2,1)S(1)}, bf16[2,96,768]{2,1,0:T(8,128)(2,1)S(1)}, bf16[2,96,768]{2,1,0:T(8,128)(2,1)S(1)}) custom-call(s32[2]{0:T(128)S(1)} %pad_add_fusion.who, bf16[768,768]{1,0:T(8,128)(2,1)S(1)} %shard_map.55.perm, ...), custom_call_target="tpu_custom_call" | custom-call | bytes 6045704 | tf_op jit(solution)/shard_map/pallas_call | solution.py:324
  25.9 0.0 collective-permute-done.w_in
  25.9 0.1 collective-permute-start.4
  26.0 3.3 %collective-permute-start.5 = (f32[2,768]{1,0:T(2,128)S(1)}, f32[2,768]{1,0:T(2,128)S(1)}, u32[]{:S(2)}, u32[]{:S(2)}) collective-permute-start(f32[2,768]{1,0:T(2,128)S(1)} %get-tuple-element.87.refs_0_), channel_id=1, source_target_pairs={{0,8},{8,0},{1,9},{9,1},{16,24},{24,16},{17,25},{25,17}} | collective-permute-start | bytes 18440 | tf_op jit(solution)/shard_map/ppermute | solution.py:383
  29.3 0.0 copy-done.3
  29.3 0.0 collective-permute-done.4.w_swapped
  29.4 0.0 copy-done
  29.4 3.2 %shard_map.61.d_ref = f32[2,96,96]{2,1,0:T(8,128)S(1)} custom-call(s32[2]{0:T(128)S(1)} %pad_add_fusion.who, bf16[768,768]{1,0:T(8,128)(2,1)S(1)} %bitcast.5, bf16[384,768]{1,0:T(8,128)(2,1)S(1)} %collective-permute-done.w_in, bf16[384,768]{1,0:T(8,128)(2,1)S(1)} %collective-permute-done.4.w_swapped, bf16[2,192,768]{2,1,0:T(8,128)(2,1)S(1)} %get-tuple-element.82.ap, ...), custom_call_target="tpu_custom_call" | custom-call | bytes 4202504 | tf_op jit(solution)/shard_map/pallas_call | solution.py:324
  32.5 0.0 collective-permute-done.5.refs_1_
  32.5 1.1 %shard_map.62 = (f32[6,128]{1,0:T(8,128)S(1)}, f32[6,128]{1,0:T(8,128)S(1)}, f32[6,128]{1,0:T(8,128)S(1)}) custom-call(s32[2]{0:T(128)S(1)} %pad_add_fusion.who, f32[2,96,96]{2,1,0:T(8,128)S(1)} %shard_map.61.d_ref, bf16[2,96,768]{2,1,0:T(8,128)(2,1)S(1)} %get-tuple-element.84.v, bf16[2,96,768]{2,1,0:T(8,128)(2,1)S(1)} %get-tuple-element.85.ca, ...), custom_call_target="tpu_custom_call" | custom-call | bytes 983048 | tf_op jit(solution)/shard_map/pallas_call | solution.py:324
  33.7 2.7 %collective-permute-start.6 = (f32[6,128]{1,0:T(8,128)S(1)}, f32[6,128]{1,0:T(8,128)S(1)}, u32[]{:S(2)}, u32[]{:S(2)}) collective-permute-start(f32[6,128]{1,0:T(8,128)S(1)} %get-tuple-element.89), channel_id=1, source_target_pairs={{0,2},{1,5},{2,0},{3,7},{4,1},{5,13},{6,3},{7,15},{8,10},{9,14},{1... | collective-permute-start | bytes 9224 | tf_op jit(solution)/shard_map/ppermute | solution.py:347
  36.3 0.7 %collective-permute-start.7 = (f32[6,128]{1,0:T(8,128)S(1)}, f32[6,128]{1,0:T(8,128)S(1)}, u32[]{:S(2)}, u32[]{:S(2)}) collective-permute-start(f32[6,128]{1,0:T(8,128)S(1)} %get-tuple-element.90), channel_id=1, source_target_pairs={{1,7},{3,5},{5,9},{7,11},{9,13},{11,15},{17,23},{19,21},{21,25},{2... | collective-permute-start | bytes 9224 | tf_op jit(solution)/shard_map/ppermute | solution.py:347
  37.0 2.2 %collective-permute-done.6 = f32[6,128]{1,0:T(8,128)S(1)} collective-permute-done((f32[6,128]{1,0:T(8,128)S(1)}, f32[6,128]{1,0:T(8,128)S(1)}, u32[]{:S(2)}, u32[]{:S(2)}) %collective-permute-start.6) | collective-permute-done | bytes 3104 | tf_op jit(solution)/shard_map/ppermute | solution.py:347
  39.2 0.0 collective-permute-done.7
  39.2 0.0 collective-permute-start.8
  39.2 1.2 %collective-permute-done.8 = f32[6,128]{1,0:T(8,128)S(1)} collective-permute-done((f32[6,128]{1,0:T(8,128)S(1)}, f32[6,128]{1,0:T(8,128)S(1)}, u32[]{:S(2)}, u32[]{:S(2)}) %collective-permute-start.8) | collective-permute-done | bytes 3104 | tf_op jit(solution)/shard_map/ppermute | solution.py:350
  40.3 0.6 %add.15 = f32[6,128]{1,0:T(8,128)} add(f32[6,128]{1,0:T(8,128)S(1)} %add_add_fusion, f32[6,128]{1,0:T(8,128)S(1)} %collective-permute-done.8) | non-fusion elementwise | flops 768 | bytes 9216 | tf_op jit(solution)/shard_map/add | solution.py:411
  (3 shorter events, 0.1 us)
Async XLA Ops:
  0.0 11.6 %copy-start.1 = (s32[3,768]{1,0:T(4,128)S(1)}, s32[3,768]{1,0:T(4,128)}, u32[]{:S(2)}) copy-start(s32[3,768]{1,0:T(4,128)} %umk.1) | copy-start | bytes 27652
  1.1 0.7 %copy-start.2 = (f32[6,128]{1,0:T(8,128)S(1)}, f32[6,128]{1,0:T(8,128)}, u32[]{:S(2)}) copy-start(f32[6,128]{1,0:T(8,128)} %hay.1) | copy-start | bytes 9220
  1.8 12.5 %collective-permute-start.1 = (bf16[208,768]{1,0:T(8,128)(2,1)S(1)}, bf16[208,768]{1,0:T(8,128)(2,1)S(1)}, u32[]{:S(2)}, u32[]{:S(2)}) collective-permute-start(bf16[208,768]{1,0:T(8,128)(2,1)S(1)} %get-tuple-element.48.refs_0_), channel_id=1, source_target_pairs={{6,0},{3,1},{0,2},{5,3},{1,4},{13,5},{2,6},{15,7},{10,8},{14,9},{7... | collective-permute-start | bytes 958472 | tf_op jit(solution)/shard_map/ppermute | solution.py:347
  7.8 18.1 %collective-permute-start = (bf16[384,768]{1,0:T(8,128)(2,1)S(1)}, bf16[384,768]{1,0:T(8,128)(2,1)S(1)}, u32[]{:S(2)}, u32[]{:S(2)}) collective-permute-start(bf16[384,768]{1,0:T(8,128)(2,1)S(1)} %dynamic-slice_bitcast_fusion), channel_id=1, source_target_pairs={{0,8},{2,10},{4,6},{1,9},{3,11},{5,7},{16,24},{18,26},{20,22},{17,... | collective-permute-start | bytes 1769480 | tf_op jit(solution)/shard_map/ppermute | solution.py:370
  10.2 12.6 %collective-permute-start.2 = (bf16[224,768]{1,0:T(8,128)(2,1)S(1)}, bf16[224,768]{1,0:T(8,128)(2,1)S(1)}, u32[]{:S(2)}, u32[]{:S(2)}) collective-permute-start(bf16[224,768]{1,0:T(8,128)(2,1)S(1)} %get-tuple-element.60), channel_id=1, source_target_pairs={{4,0},{5,1},{14,2},{7,3},{9,5},{11,7},{12,8},{13,9},{8,10},{15,11}... | collective-permute-start | bytes 1032200 | tf_op jit(solution)/shard_map/ppermute | solution.py:347
  14.4 1.7 %collective-permute-start.3 = (bf16[208,768]{1,0:T(8,128)(2,1)S(1)}, bf16[208,768]{1,0:T(8,128)(2,1)S(1)}, u32[]{:S(2)}, u32[]{:S(2)}) collective-permute-start(bf16[208,768]{1,0:T(8,128)(2,1)S(1)} %collective-permute-done.1.refs_0_), channel_id=1, source_target_pairs={{0,1},{1,0},{2,3},{3,2},{4,5},{5,4},{6,7},{7,6},{8,9},{9,8},{10,11... | collective-permute-start | bytes 958472 | tf_op jit(solution)/shard_map/ppermute | solution.py:350
  24.1 5.2 %copy-start.3 = (f32[768]{0:T(1024)S(1)}, f32[768]{0:T(1024)}, u32[]{:S(2)}) copy-start(f32[768]{0:T(1024)} %param.8) | copy-start | bytes 9220
  24.1 5.2 %copy-start = (bf16[1,768,768]{2,1,0:T(8,128)(2,1)S(1)}, bf16[1,768,768]{2,1,0:T(8,128)(2,1)}, u32[]{:S(2)}) copy-start(bf16[1,768,768]{2,1,0:T(8,128)(2,1)} %param.7) | copy-start | bytes 3538948
  25.9 3.4 %collective-permute-start.4 = (bf16[384,768]{1,0:T(8,128)(2,1)S(1)}, bf16[384,768]{1,0:T(8,128)(2,1)S(1)}, u32[]{:S(2)}, u32[]{:S(2)}) collective-permute-start(bf16[384,768]{1,0:T(8,128)(2,1)S(1)} %collective-permute-done.w_in), channel_id=1, source_target_pairs={{0,1},{1,0},{2,3},{3,2},{4,5},{5,4},{6,7},{7,6},{8,9},{9,8},{10,11... | collective-permute-start | bytes 1769480 | tf_op jit(solution)/shard_map/ppermute | solution.py:350
  26.0 6.5 %collective-permute-start.5 = (f32[2,768]{1,0:T(2,128)S(1)}, f32[2,768]{1,0:T(2,128)S(1)}, u32[]{:S(2)}, u32[]{:S(2)}) collective-permute-start(f32[2,768]{1,0:T(2,128)S(1)} %get-tuple-element.87.refs_0_), channel_id=1, source_target_pairs={{0,8},{8,0},{1,9},{9,1},{16,24},{24,16},{17,25},{25,17}} | collective-permute-start | bytes 18440 | tf_op jit(solution)/shard_map/ppermute | solution.py:383
  33.7 5.5 %collective-permute-start.6 = (f32[6,128]{1,0:T(8,128)S(1)}, f32[6,128]{1,0:T(8,128)S(1)}, u32[]{:S(2)}, u32[]{:S(2)}) collective-permute-start(f32[6,128]{1,0:T(8,128)S(1)} %get-tuple-element.89), channel_id=1, source_target_pairs={{0,2},{1,5},{2,0},{3,7},{4,1},{5,13},{6,3},{7,15},{8,10},{9,14},{1... | collective-permute-start | bytes 9224 | tf_op jit(solution)/shard_map/ppermute | solution.py:347
  36.3 2.8 %collective-permute-start.7 = (f32[6,128]{1,0:T(8,128)S(1)}, f32[6,128]{1,0:T(8,128)S(1)}, u32[]{:S(2)}, u32[]{:S(2)}) collective-permute-start(f32[6,128]{1,0:T(8,128)S(1)} %get-tuple-element.90), channel_id=1, source_target_pairs={{1,7},{3,5},{5,9},{7,11},{9,13},{11,15},{17,23},{19,21},{21,25},{2... | collective-permute-start | bytes 9224 | tf_op jit(solution)/shard_map/ppermute | solution.py:347
  39.2 1.2 %collective-permute-start.8 = (f32[6,128]{1,0:T(8,128)S(1)}, f32[6,128]{1,0:T(8,128)S(1)}, u32[]{:S(2)}, u32[]{:S(2)}) collective-permute-start(f32[6,128]{1,0:T(8,128)S(1)} %add_add_fusion), channel_id=1, source_target_pairs={{0,1},{1,0},{2,3},{3,2},{4,5},{5,4},{6,7},{7,6},{8,9},{9,8},{10,11... | collective-permute-start | bytes 9224 | tf_op jit(solution)/shard_map/ppermute | solution.py:350

commit v2 on v1

--- a/solution.py
+++ b/solution.py
@@ -184,26 +184,21 @@
         permute(a_scr, ca, perm, [ap.at[j] for j in each], [wt.at[j] for j in each], [cb.at[j] for j in each])
 
 
-def last_kernel(who, msg, earlier, v, c, a, xs):
+def pick_kernel(who, perm, msg, earlier, *refs):
+    own, two = refs[0:5], refs[5:10]
+    ap_ref, wt_ref, vt_ref, ca_ref, cb_ref, xs, ap_3, wt_3, v_3, c_3, cb_3, a_3 = refs[10:]
+    rows = v_3.shape[0]
+
     @pl.when(entry(who, 0) == 1)
     def _():
-        amp, turned = amplitude(msg, v, c)
-        a[...] = amp.astype(BF)
-        xs[...] = earlier[...] + sums(c, amp, turned)
+        amp, turned = amplitude(msg, v_3, c_3)
+        a_3[...] = amp.astype(BF)
+        xs[...] = earlier[...] + sums(c_3, amp, turned)
+        permute(a_3, c_3, perm, [ap_3], [wt_3], [cb_3])
 
     @pl.when(entry(who, 0) == 0)
     def _():
         xs[...] = jnp.zeros_like(xs)
-
-
-def pick_kernel(who, perm, *refs):
-    own, two, (v_3, c_3, a_3) = refs[0:5], refs[5:10], refs[10:13]
-    ap_ref, wt_ref, vt_ref, ca_ref, cb_ref, ap_3, wt_3, cb_3 = refs[13:]
-    rows = v_3.shape[0]
-
-    @pl.when(entry(who, 0) == 1)
-    def _():
-        permute(a_3, c_3, perm, [ap_3], [wt_3], [cb_3])
 
     def held(slot):
         if slot == 3:
@@ -378,23 +373,18 @@
     got_2 = over_cores(again, FETCH_ROUNDS[1])
     two = prep(perm, [got_1, swap(got_1)], [own[5]], known=False)
     got_2, *two = lax.optimization_barrier((got_2, *two))
-    bands = shape((rows, planes), BF)
-    v_3, c_3, a_3, xs = call(last_kernel, [bands, bands, bands, shape((2, planes), F32)], [who, got_2, two[5]])
-    xs_in = lax.ppermute(xs, "blk", SUMS)
     total_k = kr * lax.axis_size("blk")
     scale_exchange = 1.0 / (8.0 * math.sqrt(planes * total_k))
     scale_direct = -1.0 / (8.0 * math.sqrt(planes * kr * (STOPS + 1)))
     item = shape((2, rows, planes), BF)
-    ap, wt, v, ca, cb = call(
+    bands = pltpu.VMEM((rows, planes), BF)
+    ap, wt, v, ca, cb, xs = call(
         pick_kernel,
-        [shape((2, 2 * rows, planes), BF), shape((2, planes, rows), BF), item, item, item],
-        [who, perm, *own[:5], *two[:5], v_3, c_3, a_3],
-        scratch=[
-            pltpu.VMEM((2 * rows, planes), BF),
-            pltpu.VMEM((planes, rows), BF),
-            pltpu.VMEM((rows, planes), BF),
-        ],
+        [shape((2, 2 * rows, planes), BF), shape((2, planes, rows), BF), item, item, item, shape((2, planes), F32)],
+        [who, perm, got_2, two[5], *own[:5], *two[:5]],
+        scratch=[pltpu.VMEM((2 * rows, planes), BF), pltpu.VMEM((planes, rows), BF), bands, bands, bands, bands],
     )
+    xs_in = lax.ppermute(xs, "blk", SUMS)
     w_in, ap, wt = lax.optimization_barrier((w_in, ap, wt))
     (d,) = call(
         main_kernel,

time: 41.3 us -> 40.5 us (0.981)
  Pallas kernels: 12.7 us -> 11.9 us
    pallas_call x8 -> x7, Pallas kernels: 12.7 us -> 11.9 us  [call(): pl.pallas_call(kernel, out_shape=outs, in_specs=specs, out_specs=[VM] * l...]
  transfers between devices with their start and end apart: 9 -> 9, of which waited for: 4 -> 4; matrix products, arithmetic and copies ran while one was open for 3% -> 3% of each run, Pallas kernels for 28% -> 27%
where the time goes in v2:
time: 40.5 us; the launch traced here: 40.2 us
  starting transfers between devices  15.4 us (38%)
  Pallas kernels  11.9 us (29%)
  waiting for transfers between devices  9.13 us (23%)
  local copies, waits for them, and re-layouts  2.89 us (7%)
  other arithmetic  0.67 us (2%)
    pallas_call x7, Pallas kernels, call(): pl.pallas_call(kernel, out_shape=outs, in_specs=specs, out_specs=[VM] * l...  11.9 us
    ppermute x4, starting transfers between devices, over_cores(): return lax.ppermute(x, ('blk', 'pair'), pairs)  9.4 us
    ppermute x4, waiting for transfers between devices, over_cores(): return lax.ppermute(x, ('blk', 'pair'), pairs)  6.36 us
    ppermute x1, starting transfers between devices, eight_blocks(): xs_in = lax.ppermute(xs, 'blk', SUMS)  3.41 us
    ppermute x3, waiting for transfers between devices, swap(): return lax.ppermute(x, 'pair', [(0, 1), (1, 0)])  2.77 us
    ppermute x1, starting transfers between devices, eight_blocks(): lax.ppermute(lax.dynamic_slice_in_dim(screened[0], member * gh, gh, 0), '...  2.42 us
    dynamic_slice x1, local copies, waits for them, and re-layouts, eight_blocks(): lax.dynamic_slice_in_dim(screened[0], member * gh, gh, 0)  1.11 us
    reshape x1, local copies, waits for them, and re-layouts, eight_blocks(): flat = wavefunc.reshape(kr * nb * 2, planes)  1.09 us
  transfers between devices with their start and end apart: 9, of which 4 were waited for; matrix products, arithmetic and copies ran while one was open for 3% of the time, Pallas kernels for 27%

profile of v2, /device:TPU:0, one launch (start us, length us, event | category | flops | bytes accessed | tf_op | source)
XLA Modules:
  0.0 40.2 jit_solution(3136494632952203336)
XLA Ops:
  0.0 0.0 copy-start.1
  0.0 1.1 %reshape.7.flat = bf16[192,768]{1,0:T(8,128)(2,1)S(1)} reshape(bf16[6,16,2,768]{3,2,1,0:T(2,128)(2,1)} %param.5) | data formatting | bytes 589824 | tf_op jit(solution)/shard_map/reshape | solution.py:366
  1.1 0.0 copy-start.2
  1.1 0.7 %copy-done.2 = f32[6,128]{1,0:T(8,128)S(1)} copy-done((f32[6,128]{1,0:T(8,128)S(1)}, f32[6,128]{1,0:T(8,128)}, u32[]{:S(2)}) %copy-start.2) | copy-done | bytes 3096
  1.8 4.8 %collective-permute-start.2 = (bf16[208,768]{1,0:T(8,128)(2,1)S(1)}, bf16[208,768]{1,0:T(8,128)(2,1)S(1)}, u32[]{:S(2)}, u32[]{:S(2)}) collective-permute-start(bf16[208,768]{1,0:T(8,128)(2,1)S(1)} %get-tuple-element.46.refs_0_), channel_id=1, source_target_pairs={{6,0},{3,1},{0,2},{5,3},{1,4},{13,5},{2,6},{15,7},{10,8},{14,9},{7... | collective-permute-start | bytes 958472 | tf_op jit(solution)/shard_map/ppermute | solution.py:342
  6.7 1.1 %dynamic-slice_bitcast_fusion = bf16[384,768]{1,0:T(8,128)(2,1)S(1)} fusion(bf16[1,768,768]{2,1,0:T(8,128)(2,1)} %param.7, s32[]{:T(128)S(6)} %select_n.3), kind=kLoop, calls=%fused_computation | loop fusion | bytes 1179652 | tf_op jit(solution)/shard_map/dynamic_slice | solution.py:365
  7.8 2.4 %collective-permute-start = (bf16[384,768]{1,0:T(8,128)(2,1)S(1)}, bf16[384,768]{1,0:T(8,128)(2,1)S(1)}, u32[]{:S(2)}, u32[]{:S(2)}) collective-permute-start(bf16[384,768]{1,0:T(8,128)(2,1)S(1)} %dynamic-slice_bitcast_fusion), channel_id=1, source_target_pairs={{0,8},{2,10},{4,6},{1,9},{3,11},{5,7},{16,24},{18,26},{20,22},{17,... | collective-permute-start | bytes 1769480 | tf_op jit(solution)/shard_map/ppermute | solution.py:365
  10.2 1.3 %collective-permute-start.1 = (bf16[224,768]{1,0:T(8,128)(2,1)S(1)}, bf16[224,768]{1,0:T(8,128)(2,1)S(1)}, u32[]{:S(2)}, u32[]{:S(2)}) collective-permute-start(bf16[224,768]{1,0:T(8,128)(2,1)S(1)} %get-tuple-element.45), channel_id=1, source_target_pairs={{4,0},{5,1},{14,2},{7,3},{9,5},{11,7},{12,8},{13,9},{8,10},{15,11}... | collective-permute-start | bytes 1032200 | tf_op jit(solution)/shard_map/ppermute | solution.py:342
  11.5 0.1 pad_add_fusion.who
  11.6 0.0 copy-done.1
  11.6 0.8 %shard_map.55.perm = bf16[768,768]{1,0:T(8,128)(2,1)S(1)} custom-call(s32[2]{0:T(128)S(1)} %pad_add_fusion.who, s32[3,768]{1,0:T(4,128)S(1)} %copy-done.1), custom_call_target="tpu_custom_call" | custom-call | bytes 1188872 | tf_op jit(solution)/shard_map/pallas_call | solution.py:319
  12.4 2.0 %shard_map.57 = (bf16[1,192,768]{2,1,0:T(8,128)(2,1)S(1)}, bf16[1,768,96]{2,1,0:T(8,128)(2,1)S(1)}, bf16[1,96,768]{2,1,0:T(8,128)(2,1)S(1)}, bf16[96,768]{1,0:T(...) custom-call(s32[2]{0:T(128)S(1)} %pad_add_fusion.who, bf16[768,768]{1,0:T(8,128)(2,1)S(1)} %shard_map.55.perm, ...), custom_call_target="tpu_custom_call" | custom-call | bytes 2390024 | tf_op jit(solution)/shard_map/pallas_call | solution.py:319
  14.4 0.0 collective-permute-done.2.refs_0_
  14.4 0.1 collective-permute-start.3
  14.4 1.6 %collective-permute-done.3.refs_1_ = bf16[208,768]{1,0:T(8,128)(2,1)S(1)} collective-permute-done((bf16[208,768]{1,0:T(8,128)(2,1)S(1)}, bf16[208,768]{1,0:T(8,128)(2,1)S(1)}, u32[]{:S(2)}, u32[]{:S(2)}) %collective-permute-start.3) | collective-permute-done | bytes 319520 | tf_op jit(solution)/shard_map/ppermute | solution.py:345
  16.0 2.7 %shard_map.58 = (bf16[2,192,768]{2,1,0:T(8,128)(2,1)S(1)}, bf16[2,768,96]{2,1,0:T(8,128)(2,1)S(1)}, bf16[2,96,768]{2,1,0:T(8,128)(2,1)S(1)}, bf16[192,768]{1,0:T...) custom-call(s32[2]{0:T(128)S(1)} %pad_add_fusion.who, bf16[768,768]{1,0:T(8,128)(2,1)S(1)} %shard_map.55.perm, ...), custom_call_target="tpu_custom_call" | custom-call | tf_op jit(solution)/shard_map/pallas_call | solution.py:319
  18.7 4.1 %collective-permute-done.1.msg = bf16[224,768]{1,0:T(8,128)(2,1)S(1)} collective-permute-done((bf16[224,768]{1,0:T(8,128)(2,1)S(1)}, bf16[224,768]{1,0:T(8,128)(2,1)S(1)}, u32[]{:S(2)}, u32[]{:S(2)}) %collective-permute-start.1) | collective-permute-done | bytes 344096 | tf_op jit(solution)/shard_map/ppermute | solution.py:342
  22.9 0.0 copy-start.3
  22.9 0.0 copy-start
  22.9 2.2 %shard_map.59 = (bf16[2,192,768]{2,1,0:T(8,128)(2,1)S(1)}, bf16[2,768,96]{2,1,0:T(8,128)(2,1)S(1)}, bf16[2,96,768]{2,1,0:T(8,128)(2,1)S(1)}, bf16[2,96,768]{2,1,...) custom-call(s32[2]{0:T(128)S(1)} %pad_add_fusion.who, bf16[768,768]{1,0:T(8,128)(2,1)S(1)} %shard_map.55.perm, ...), custom_call_target="tpu_custom_call" | custom-call | bytes 5959688 | tf_op jit(solution)/shard_map/pallas_call | solution.py:319
  25.1 0.0 collective-permute-done.w_in
  25.1 0.1 collective-permute-start.4
  25.2 3.4 %collective-permute-start.5 = (f32[2,768]{1,0:T(2,128)S(1)}, f32[2,768]{1,0:T(2,128)S(1)}, u32[]{:S(2)}, u32[]{:S(2)}) collective-permute-start(f32[2,768]{1,0:T(2,128)S(1)} %get-tuple-element.81.refs_0_), channel_id=1, source_target_pairs={{0,8},{8,0},{1,9},{9,1},{16,24},{24,16},{17,25},{25,17}} | collective-permute-start | bytes 18440 | tf_op jit(solution)/shard_map/ppermute | solution.py:387
  28.6 0.0 copy-done.3
  28.6 0.0 collective-permute-done.4.w_swapped
  28.6 0.0 copy-done
  28.6 3.1 %shard_map.60.d_ref = f32[2,96,96]{2,1,0:T(8,128)S(1)} custom-call(s32[2]{0:T(128)S(1)} %pad_add_fusion.who, bf16[768,768]{1,0:T(8,128)(2,1)S(1)} %bitcast.5, bf16[384,768]{1,0:T(8,128)(2,1)S(1)} %collective-permute-done.w_in, bf16[384,768]{1,0:T(8,128)(2,1)S(1)} %collective-permute-done.4.w_swapped, bf16[2,192,768]{2,1,0:T(8,128)(2,1)S(1)} %get-tuple-element.76.ap, ...), custom_call_target="tpu_custom_call" | custom-call | bytes 4202504 | tf_op jit(solution)/shard_map/pallas_call | solution.py:319
  31.8 0.0 collective-permute-done.5.refs_1_
  31.8 1.1 %shard_map.61 = (f32[6,128]{1,0:T(8,128)S(1)}, f32[6,128]{1,0:T(8,128)S(1)}, f32[6,128]{1,0:T(8,128)S(1)}) custom-call(s32[2]{0:T(128)S(1)} %pad_add_fusion.who, f32[2,96,96]{2,1,0:T(8,128)S(1)} %shard_map.60.d_ref, bf16[2,96,768]{2,1,0:T(8,128)(2,1)S(1)} %get-tuple-element.78.v, bf16[2,96,768]{2,1,0:T(8,128)(2,1)S(1)} %get-tuple-element.79.ca, ...), custom_call_target="tpu_custom_call" | custom-call | bytes 983048 | tf_op jit(solution)/shard_map/pallas_call | solution.py:319
  32.9 2.6 %collective-permute-start.6 = (f32[6,128]{1,0:T(8,128)S(1)}, f32[6,128]{1,0:T(8,128)S(1)}, u32[]{:S(2)}, u32[]{:S(2)}) collective-permute-start(f32[6,128]{1,0:T(8,128)S(1)} %get-tuple-element.83), channel_id=1, source_target_pairs={{0,2},{1,5},{2,0},{3,7},{4,1},{5,13},{6,3},{7,15},{8,10},{9,14},{1... | collective-permute-start | bytes 9224 | tf_op jit(solution)/shard_map/ppermute | solution.py:342
  35.5 0.7 %collective-permute-start.7 = (f32[6,128]{1,0:T(8,128)S(1)}, f32[6,128]{1,0:T(8,128)S(1)}, u32[]{:S(2)}, u32[]{:S(2)}) collective-permute-start(f32[6,128]{1,0:T(8,128)S(1)} %get-tuple-element.84), channel_id=1, source_target_pairs={{1,7},{3,5},{5,9},{7,11},{9,13},{11,15},{17,23},{19,21},{21,25},{2... | collective-permute-start | bytes 9224 | tf_op jit(solution)/shard_map/ppermute | solution.py:342
  36.2 2.2 %collective-permute-done.6 = f32[6,128]{1,0:T(8,128)S(1)} collective-permute-done((f32[6,128]{1,0:T(8,128)S(1)}, f32[6,128]{1,0:T(8,128)S(1)}, u32[]{:S(2)}, u32[]{:S(2)}) %collective-permute-start.6) | collective-permute-done | bytes 3104 | tf_op jit(solution)/shard_map/ppermute | solution.py:342
  38.4 0.0 collective-permute-done.7
  38.4 0.0 collective-permute-start.8
  38.4 1.2 %collective-permute-done.8 = f32[6,128]{1,0:T(8,128)S(1)} collective-permute-done((f32[6,128]{1,0:T(8,128)S(1)}, f32[6,128]{1,0:T(8,128)S(1)}, u32[]{:S(2)}, u32[]{:S(2)}) %collective-permute-start.8) | collective-permute-done | bytes 3104 | tf_op jit(solution)/shard_map/ppermute | solution.py:345
  39.6 0.6 %add.15 = f32[6,128]{1,0:T(8,128)} add(f32[6,128]{1,0:T(8,128)S(1)} %add_add_fusion, f32[6,128]{1,0:T(8,128)S(1)} %collective-permute-done.8) | non-fusion elementwise | flops 768 | bytes 9216 | tf_op jit(solution)/shard_map/add | solution.py:401
  (3 shorter events, 0.1 us)
Async XLA Ops:
  0.0 11.6 %copy-start.1 = (s32[3,768]{1,0:T(4,128)S(1)}, s32[3,768]{1,0:T(4,128)}, u32[]{:S(2)}) copy-start(s32[3,768]{1,0:T(4,128)} %umk.1) | copy-start | bytes 27652
  1.1 0.7 %copy-start.2 = (f32[6,128]{1,0:T(8,128)S(1)}, f32[6,128]{1,0:T(8,128)}, u32[]{:S(2)}) copy-start(f32[6,128]{1,0:T(8,128)} %hay.1) | copy-start | bytes 9220
  1.8 12.5 %collective-permute-start.2 = (bf16[208,768]{1,0:T(8,128)(2,1)S(1)}, bf16[208,768]{1,0:T(8,128)(2,1)S(1)}, u32[]{:S(2)}, u32[]{:S(2)}) collective-permute-start(bf16[208,768]{1,0:T(8,128)(2,1)S(1)} %get-tuple-element.46.refs_0_), channel_id=1, source_target_pairs={{6,0},{3,1},{0,2},{5,3},{1,4},{13,5},{2,6},{15,7},{10,8},{14,9},{7... | collective-permute-start | bytes 958472 | tf_op jit(solution)/shard_map/ppermute | solution.py:342
  7.8 17.3 %collective-permute-start = (bf16[384,768]{1,0:T(8,128)(2,1)S(1)}, bf16[384,768]{1,0:T(8,128)(2,1)S(1)}, u32[]{:S(2)}, u32[]{:S(2)}) collective-permute-start(bf16[384,768]{1,0:T(8,128)(2,1)S(1)} %dynamic-slice_bitcast_fusion), channel_id=1, source_target_pairs={{0,8},{2,10},{4,6},{1,9},{3,11},{5,7},{16,24},{18,26},{20,22},{17,... | collective-permute-start | bytes 1769480 | tf_op jit(solution)/shard_map/ppermute | solution.py:365
  10.2 12.6 %collective-permute-start.1 = (bf16[224,768]{1,0:T(8,128)(2,1)S(1)}, bf16[224,768]{1,0:T(8,128)(2,1)S(1)}, u32[]{:S(2)}, u32[]{:S(2)}) collective-permute-start(bf16[224,768]{1,0:T(8,128)(2,1)S(1)} %get-tuple-element.45), channel_id=1, source_target_pairs={{4,0},{5,1},{14,2},{7,3},{9,5},{11,7},{12,8},{13,9},{8,10},{15,11}... | collective-permute-start | bytes 1032200 | tf_op jit(solution)/shard_map/ppermute | solution.py:342
  14.4 1.7 %collective-permute-start.3 = (bf16[208,768]{1,0:T(8,128)(2,1)S(1)}, bf16[208,768]{1,0:T(8,128)(2,1)S(1)}, u32[]{:S(2)}, u32[]{:S(2)}) collective-permute-start(bf16[208,768]{1,0:T(8,128)(2,1)S(1)} %collective-permute-done.2.refs_0_), channel_id=1, source_target_pairs={{0,1},{1,0},{2,3},{3,2},{4,5},{5,4},{6,7},{7,6},{8,9},{9,8},{10,11... | collective-permute-start | bytes 958472 | tf_op jit(solution)/shard_map/ppermute | solution.py:345
  22.9 5.7 %copy-start.3 = (f32[768]{0:T(1024)S(1)}, f32[768]{0:T(1024)}, u32[]{:S(2)}) copy-start(f32[768]{0:T(1024)} %param.8) | copy-start | bytes 9220
  22.9 5.8 %copy-start = (bf16[1,768,768]{2,1,0:T(8,128)(2,1)S(1)}, bf16[1,768,768]{2,1,0:T(8,128)(2,1)}, u32[]{:S(2)}) copy-start(bf16[1,768,768]{2,1,0:T(8,128)(2,1)} %param.7) | copy-start | bytes 3538948
  25.1 3.5 %collective-permute-start.4 = (bf16[384,768]{1,0:T(8,128)(2,1)S(1)}, bf16[384,768]{1,0:T(8,128)(2,1)S(1)}, u32[]{:S(2)}, u32[]{:S(2)}) collective-permute-start(bf16[384,768]{1,0:T(8,128)(2,1)S(1)} %collective-permute-done.w_in), channel_id=1, source_target_pairs={{0,1},{1,0},{2,3},{3,2},{4,5},{5,4},{6,7},{7,6},{8,9},{9,8},{10,11... | collective-permute-start | bytes 1769480 | tf_op jit(solution)/shard_map/ppermute | solution.py:345
  25.2 6.6 %collective-permute-start.5 = (f32[2,768]{1,0:T(2,128)S(1)}, f32[2,768]{1,0:T(2,128)S(1)}, u32[]{:S(2)}, u32[]{:S(2)}) collective-permute-start(f32[2,768]{1,0:T(2,128)S(1)} %get-tuple-element.81.refs_0_), channel_id=1, source_target_pairs={{0,8},{8,0},{1,9},{9,1},{16,24},{24,16},{17,25},{25,17}} | collective-permute-start | bytes 18440 | tf_op jit(solution)/shard_map/ppermute | solution.py:387
  32.9 5.5 %collective-permute-start.6 = (f32[6,128]{1,0:T(8,128)S(1)}, f32[6,128]{1,0:T(8,128)S(1)}, u32[]{:S(2)}, u32[]{:S(2)}) collective-permute-start(f32[6,128]{1,0:T(8,128)S(1)} %get-tuple-element.83), channel_id=1, source_target_pairs={{0,2},{1,5},{2,0},{3,7},{4,1},{5,13},{6,3},{7,15},{8,10},{9,14},{1... | collective-permute-start | bytes 9224 | tf_op jit(solution)/shard_map/ppermute | solution.py:342
  35.5 2.9 %collective-permute-start.7 = (f32[6,128]{1,0:T(8,128)S(1)}, f32[6,128]{1,0:T(8,128)S(1)}, u32[]{:S(2)}, u32[]{:S(2)}) collective-permute-start(f32[6,128]{1,0:T(8,128)S(1)} %get-tuple-element.84), channel_id=1, source_target_pairs={{1,7},{3,5},{5,9},{7,11},{9,13},{11,15},{17,23},{19,21},{21,25},{2... | collective-permute-start | bytes 9224 | tf_op jit(solution)/shard_map/ppermute | solution.py:342
  38.4 1.2 %collective-permute-start.8 = (f32[6,128]{1,0:T(8,128)S(1)}, f32[6,128]{1,0:T(8,128)S(1)}, u32[]{:S(2)}, u32[]{:S(2)}) collective-permute-start(f32[6,128]{1,0:T(8,128)S(1)} %add_add_fusion), channel_id=1, source_target_pairs={{0,1},{1,0},{2,3},{3,2},{4,5},{5,4},{6,7},{7,6},{8,9},{9,8},{10,11... | collective-permute-start | bytes 9224 | tf_op jit(solution)/shard_map/ppermute | solution.py:345

commit v3 on v2

--- a/solution.py
+++ b/solution.py
@@ -228,19 +228,19 @@
 
     @pl.when((entry(who, 0) == 1) & (entry(who, 2) == 0))
     def _():
-        wf[...] = w_own[...].astype(F32)
+        wf[...] = w_own[...]
 
     @pl.when((entry(who, 0) == 1) & (entry(who, 2) == 1))
     def _():
-        wf[pl.ds(pl.multiple_of(p * gh, 128), gh), :] = w_in[...].astype(F32)
-        wf[pl.ds(pl.multiple_of((1 - p) * gh, 128), gh), :] = w_swapped[...].astype(F32)
+        wf[pl.ds(pl.multiple_of(p * gh, 128), gh), :] = w_in[...]
+        wf[pl.ds(pl.multiple_of((1 - p) * gh, 128), gh), :] = w_swapped[...]
 
     @pl.when(entry(who, 0) == 1)
     def _():
         kernels = []
         for i in range(2):
             for h in range(2):
-                w = wf[h * gh : (h + 1) * gh, :]
+                w = wf[h * gh : (h + 1) * gh, :].astype(F32)
                 left = wt[i, h * gh : (h + 1) * gh, :]
                 k_re = (w * dot(left, ap[i, 0:rows, :])).astype(BF)
                 k_im = (w * dot(left, ap[i, rows : 2 * rows, :])).astype(BF)
@@ -269,14 +269,16 @@
     ra, rb = a % 2, b // 64
     qa = one(same_v & (ra == rb), jnp.where(rb == 1, -1.0, 1.0))
     qb = one(same_v & (ra != rb))
-    q = jnp.concatenate([qa, qb], axis=1)
+    q = jnp.concatenate([qa, qb], axis=1).astype(BF)
     real_row = (a % 2) == 0
     keep = (b % 8) == ((a // 2) % 8)
     block = (iota((rows, rows), 0) // 16) == (iota((rows, rows), 1) // 16)
 
     def result(d):
         d = jnp.where(block, d, 0.0)
-        z = dot(d, q, precision=lax.Precision.HIGHEST)
+        hi = d.astype(BF)
+        lo = (d - hi.astype(F32)).astype(BF)
+        z = dot(hi, q) + dot(lo, q)
         z = jnp.where(keep, jnp.where(real_row, z[:, :128], z[:, 128:]), 0.0)
         return jnp.sum(z.reshape(kr, 16, 128), axis=1)
 
@@ -390,7 +392,7 @@
         main_kernel,
         [shape((2, rows, rows), F32)],
         [who, screened[0], w_in, swap(w_in), ap, wt, v, ca, cb],
-        scratch=[pltpu.VMEM((planes, planes), F32)],
+        scratch=[pltpu.VMEM((planes, planes), BF)],
     )
     stays, goes_1, goes_2 = call(
         functools.partial(finish_kernel, scale_direct, scale_exchange),

time: 40.5 us -> 40.3 us (level)
  no operation moved by 1% of the time
where the time goes in v3:
time: 40.3 us; the launch traced here: 40 us
  starting transfers between devices  15.4 us (38%)
  Pallas kernels  11.7 us (29%)
  waiting for transfers between devices  9.14 us (23%)
  local copies, waits for them, and re-layouts  2.89 us (7%)
  other arithmetic  0.67 us (2%)
    pallas_call x7, Pallas kernels, call(): pl.pallas_call(kernel, out_shape=outs, in_specs=specs, out_specs=[VM] * l...  11.7 us
    ppermute x4, starting transfers between devices, over_cores(): return lax.ppermute(x, ('blk', 'pair'), pairs)  9.39 us
    ppermute x4, waiting for transfers between devices, over_cores(): return lax.ppermute(x, ('blk', 'pair'), pairs)  6.36 us
    ppermute x1, starting transfers between devices, eight_blocks(): xs_in = lax.ppermute(xs, 'blk', SUMS)  3.41 us
    ppermute x3, waiting for transfers between devices, swap(): return lax.ppermute(x, 'pair', [(0, 1), (1, 0)])  2.77 us
    ppermute x1, starting transfers between devices, eight_blocks(): lax.ppermute(lax.dynamic_slice_in_dim(screened[0], member * gh, gh, 0), '...  2.42 us
    dynamic_slice x1, local copies, waits for them, and re-layouts, eight_blocks(): lax.dynamic_slice_in_dim(screened[0], member * gh, gh, 0)  1.11 us
    reshape x1, local copies, waits for them, and re-layouts, eight_blocks(): flat = wavefunc.reshape(kr * nb * 2, planes)  1.09 us
  transfers between devices with their start and end apart: 9, of which 4 were waited for; matrix products, arithmetic and copies ran while one was open for 3% of the time, Pallas kernels for 27%

profile of v3, /device:TPU:0, one launch (start us, length us, event | category | flops | bytes accessed | tf_op | source)
XLA Modules:
  0.0 40.0 jit_solution(14547798875557275021)
XLA Ops:
  0.0 0.0 copy-start.1
  0.0 1.1 %reshape.7.flat = bf16[192,768]{1,0:T(8,128)(2,1)S(1)} reshape(bf16[6,16,2,768]{3,2,1,0:T(2,128)(2,1)} %param.5) | data formatting | bytes 589824 | tf_op jit(solution)/shard_map/reshape | solution.py:368
  1.1 0.0 copy-start.2
  1.1 0.7 %copy-done.2 = f32[6,128]{1,0:T(8,128)S(1)} copy-done((f32[6,128]{1,0:T(8,128)S(1)}, f32[6,128]{1,0:T(8,128)}, u32[]{:S(2)}) %copy-start.2) | copy-done | bytes 3096
  1.8 4.8 %collective-permute-start.2 = (bf16[208,768]{1,0:T(8,128)(2,1)S(1)}, bf16[208,768]{1,0:T(8,128)(2,1)S(1)}, u32[]{:S(2)}, u32[]{:S(2)}) collective-permute-start(bf16[208,768]{1,0:T(8,128)(2,1)S(1)} %get-tuple-element.46.refs_0_), channel_id=1, source_target_pairs={{6,0},{3,1},{0,2},{5,3},{1,4},{13,5},{2,6},{15,7},{10,8},{14,9},{7... | collective-permute-start | bytes 958472 | tf_op jit(solution)/shard_map/ppermute | solution.py:344
  6.7 1.1 %dynamic-slice_bitcast_fusion = bf16[384,768]{1,0:T(8,128)(2,1)S(1)} fusion(bf16[1,768,768]{2,1,0:T(8,128)(2,1)} %param.7, s32[]{:T(128)S(6)} %select_n.3), kind=kLoop, calls=%fused_computation | loop fusion | bytes 1179652 | tf_op jit(solution)/shard_map/dynamic_slice | solution.py:367
  7.8 2.4 %collective-permute-start = (bf16[384,768]{1,0:T(8,128)(2,1)S(1)}, bf16[384,768]{1,0:T(8,128)(2,1)S(1)}, u32[]{:S(2)}, u32[]{:S(2)}) collective-permute-start(bf16[384,768]{1,0:T(8,128)(2,1)S(1)} %dynamic-slice_bitcast_fusion), channel_id=1, source_target_pairs={{0,8},{2,10},{4,6},{1,9},{3,11},{5,7},{16,24},{18,26},{20,22},{17,... | collective-permute-start | bytes 1769480 | tf_op jit(solution)/shard_map/ppermute | solution.py:367
  10.2 1.3 %collective-permute-start.1 = (bf16[224,768]{1,0:T(8,128)(2,1)S(1)}, bf16[224,768]{1,0:T(8,128)(2,1)S(1)}, u32[]{:S(2)}, u32[]{:S(2)}) collective-permute-start(bf16[224,768]{1,0:T(8,128)(2,1)S(1)} %get-tuple-element.45), channel_id=1, source_target_pairs={{4,0},{5,1},{14,2},{7,3},{9,5},{11,7},{12,8},{13,9},{8,10},{15,11}... | collective-permute-start | bytes 1032200 | tf_op jit(solution)/shard_map/ppermute | solution.py:344
  11.5 0.1 pad_add_fusion.who
  11.6 0.0 copy-done.1
  11.6 0.8 %shard_map.55.perm = bf16[768,768]{1,0:T(8,128)(2,1)S(1)} custom-call(s32[2]{0:T(128)S(1)} %pad_add_fusion.who, s32[3,768]{1,0:T(4,128)S(1)} %copy-done.1), custom_call_target="tpu_custom_call" | custom-call | bytes 1188872 | tf_op jit(solution)/shard_map/pallas_call | solution.py:321
  12.4 2.0 %shard_map.57 = (bf16[1,192,768]{2,1,0:T(8,128)(2,1)S(1)}, bf16[1,768,96]{2,1,0:T(8,128)(2,1)S(1)}, bf16[1,96,768]{2,1,0:T(8,128)(2,1)S(1)}, bf16[96,768]{1,0:T(...) custom-call(s32[2]{0:T(128)S(1)} %pad_add_fusion.who, bf16[768,768]{1,0:T(8,128)(2,1)S(1)} %shard_map.55.perm, ...), custom_call_target="tpu_custom_call" | custom-call | bytes 2390024 | tf_op jit(solution)/shard_map/pallas_call | solution.py:321
  14.4 0.0 collective-permute-done.2.refs_0_
  14.4 0.1 collective-permute-start.3
  14.4 1.6 %collective-permute-done.3.refs_1_ = bf16[208,768]{1,0:T(8,128)(2,1)S(1)} collective-permute-done((bf16[208,768]{1,0:T(8,128)(2,1)S(1)}, bf16[208,768]{1,0:T(8,128)(2,1)S(1)}, u32[]{:S(2)}, u32[]{:S(2)}) %collective-permute-start.3) | collective-permute-done | bytes 319520 | tf_op jit(solution)/shard_map/ppermute | solution.py:347
  16.0 2.7 %shard_map.58 = (bf16[2,192,768]{2,1,0:T(8,128)(2,1)S(1)}, bf16[2,768,96]{2,1,0:T(8,128)(2,1)S(1)}, bf16[2,96,768]{2,1,0:T(8,128)(2,1)S(1)}, bf16[192,768]{1,0:T...) custom-call(s32[2]{0:T(128)S(1)} %pad_add_fusion.who, bf16[768,768]{1,0:T(8,128)(2,1)S(1)} %shard_map.55.perm, ...), custom_call_target="tpu_custom_call" | custom-call | tf_op jit(solution)/shard_map/pallas_call | solution.py:321
  18.7 4.1 %collective-permute-done.1.msg = bf16[224,768]{1,0:T(8,128)(2,1)S(1)} collective-permute-done((bf16[224,768]{1,0:T(8,128)(2,1)S(1)}, bf16[224,768]{1,0:T(8,128)(2,1)S(1)}, u32[]{:S(2)}, u32[]{:S(2)}) %collective-permute-start.1) | collective-permute-done | bytes 344096 | tf_op jit(solution)/shard_map/ppermute | solution.py:344
  22.9 0.0 copy-start.3
  22.9 0.0 copy-start
  22.9 2.2 %shard_map.59 = (bf16[2,192,768]{2,1,0:T(8,128)(2,1)S(1)}, bf16[2,768,96]{2,1,0:T(8,128)(2,1)S(1)}, bf16[2,96,768]{2,1,0:T(8,128)(2,1)S(1)}, bf16[2,96,768]{2,1,...) custom-call(s32[2]{0:T(128)S(1)} %pad_add_fusion.who, bf16[768,768]{1,0:T(8,128)(2,1)S(1)} %shard_map.55.perm, ...), custom_call_target="tpu_custom_call" | custom-call | bytes 5959688 | tf_op jit(solution)/shard_map/pallas_call | solution.py:321
  25.1 0.0 collective-permute-done.w_in
  25.1 0.1 collective-permute-start.4
  25.2 3.4 %collective-permute-start.5 = (f32[2,768]{1,0:T(2,128)S(1)}, f32[2,768]{1,0:T(2,128)S(1)}, u32[]{:S(2)}, u32[]{:S(2)}) collective-permute-start(f32[2,768]{1,0:T(2,128)S(1)} %get-tuple-element.81.refs_0_), channel_id=1, source_target_pairs={{0,8},{8,0},{1,9},{9,1},{16,24},{24,16},{17,25},{25,17}} | collective-permute-start | bytes 18440 | tf_op jit(solution)/shard_map/ppermute | solution.py:389
  28.6 0.0 copy-done.3
  28.6 0.0 collective-permute-done.4.w_swapped
  28.6 0.0 copy-done
  28.6 3.0 %shard_map.60.d_ref = f32[2,96,96]{2,1,0:T(8,128)S(1)} custom-call(s32[2]{0:T(128)S(1)} %pad_add_fusion.who, bf16[768,768]{1,0:T(8,128)(2,1)S(1)} %bitcast.5, bf16[384,768]{1,0:T(8,128)(2,1)S(1)} %collective-permute-done.w_in, bf16[384,768]{1,0:T(8,128)(2,1)S(1)} %collective-permute-done.4.w_swapped, bf16[2,192,768]{2,1,0:T(8,128)(2,1)S(1)} %get-tuple-element.76.ap, ...), custom_call_target="tpu_custom_call" | custom-call | bytes 4202504 | tf_op jit(solution)/shard_map/pallas_call | solution.py:321
  31.7 0.0 collective-permute-done.5.refs_1_
  31.7 1.0 %shard_map.61 = (f32[6,128]{1,0:T(8,128)S(1)}, f32[6,128]{1,0:T(8,128)S(1)}, f32[6,128]{1,0:T(8,128)S(1)}) custom-call(s32[2]{0:T(128)S(1)} %pad_add_fusion.who, f32[2,96,96]{2,1,0:T(8,128)S(1)} %shard_map.60.d_ref, bf16[2,96,768]{2,1,0:T(8,128)(2,1)S(1)} %get-tuple-element.78.v, bf16[2,96,768]{2,1,0:T(8,128)(2,1)S(1)} %get-tuple-element.79.ca, ...), custom_call_target="tpu_custom_call" | custom-call | bytes 983048 | tf_op jit(solution)/shard_map/pallas_call | solution.py:321
  32.7 2.6 %collective-permute-start.6 = (f32[6,128]{1,0:T(8,128)S(1)}, f32[6,128]{1,0:T(8,128)S(1)}, u32[]{:S(2)}, u32[]{:S(2)}) collective-permute-start(f32[6,128]{1,0:T(8,128)S(1)} %get-tuple-element.83), channel_id=1, source_target_pairs={{0,2},{1,5},{2,0},{3,7},{4,1},{5,13},{6,3},{7,15},{8,10},{9,14},{1... | collective-permute-start | bytes 9224 | tf_op jit(solution)/shard_map/ppermute | solution.py:344
  35.3 0.7 %collective-permute-start.7 = (f32[6,128]{1,0:T(8,128)S(1)}, f32[6,128]{1,0:T(8,128)S(1)}, u32[]{:S(2)}, u32[]{:S(2)}) collective-permute-start(f32[6,128]{1,0:T(8,128)S(1)} %get-tuple-element.84), channel_id=1, source_target_pairs={{1,7},{3,5},{5,9},{7,11},{9,13},{11,15},{17,23},{19,21},{21,25},{2... | collective-permute-start | bytes 9224 | tf_op jit(solution)/shard_map/ppermute | solution.py:344
  36.0 2.2 %collective-permute-done.6 = f32[6,128]{1,0:T(8,128)S(1)} collective-permute-done((f32[6,128]{1,0:T(8,128)S(1)}, f32[6,128]{1,0:T(8,128)S(1)}, u32[]{:S(2)}, u32[]{:S(2)}) %collective-permute-start.6) | collective-permute-done | bytes 3104 | tf_op jit(solution)/shard_map/ppermute | solution.py:344
  38.2 0.0 collective-permute-done.7
  38.2 0.0 collective-permute-start.8
  38.2 1.2 %collective-permute-done.8 = f32[6,128]{1,0:T(8,128)S(1)} collective-permute-done((f32[6,128]{1,0:T(8,128)S(1)}, f32[6,128]{1,0:T(8,128)S(1)}, u32[]{:S(2)}, u32[]{:S(2)}) %collective-permute-start.8) | collective-permute-done | bytes 3104 | tf_op jit(solution)/shard_map/ppermute | solution.py:347
  39.4 0.6 %add.15 = f32[6,128]{1,0:T(8,128)} add(f32[6,128]{1,0:T(8,128)S(1)} %add_add_fusion, f32[6,128]{1,0:T(8,128)S(1)} %collective-permute-done.8) | non-fusion elementwise | flops 768 | bytes 9216 | tf_op jit(solution)/shard_map/add | solution.py:403
  (3 shorter events, 0.1 us)
Async XLA Ops:
  0.0 11.6 %copy-start.1 = (s32[3,768]{1,0:T(4,128)S(1)}, s32[3,768]{1,0:T(4,128)}, u32[]{:S(2)}) copy-start(s32[3,768]{1,0:T(4,128)} %umk.1) | copy-start | bytes 27652
  1.1 0.7 %copy-start.2 = (f32[6,128]{1,0:T(8,128)S(1)}, f32[6,128]{1,0:T(8,128)}, u32[]{:S(2)}) copy-start(f32[6,128]{1,0:T(8,128)} %hay.1) | copy-start | bytes 9220
  1.8 12.5 %collective-permute-start.2 = (bf16[208,768]{1,0:T(8,128)(2,1)S(1)}, bf16[208,768]{1,0:T(8,128)(2,1)S(1)}, u32[]{:S(2)}, u32[]{:S(2)}) collective-permute-start(bf16[208,768]{1,0:T(8,128)(2,1)S(1)} %get-tuple-element.46.refs_0_), channel_id=1, source_target_pairs={{6,0},{3,1},{0,2},{5,3},{1,4},{13,5},{2,6},{15,7},{10,8},{14,9},{7... | collective-permute-start | bytes 958472 | tf_op jit(solution)/shard_map/ppermute | solution.py:344
  7.8 17.3 %collective-permute-start = (bf16[384,768]{1,0:T(8,128)(2,1)S(1)}, bf16[384,768]{1,0:T(8,128)(2,1)S(1)}, u32[]{:S(2)}, u32[]{:S(2)}) collective-permute-start(bf16[384,768]{1,0:T(8,128)(2,1)S(1)} %dynamic-slice_bitcast_fusion), channel_id=1, source_target_pairs={{0,8},{2,10},{4,6},{1,9},{3,11},{5,7},{16,24},{18,26},{20,22},{17,... | collective-permute-start | bytes 1769480 | tf_op jit(solution)/shard_map/ppermute | solution.py:367
  10.2 12.6 %collective-permute-start.1 = (bf16[224,768]{1,0:T(8,128)(2,1)S(1)}, bf16[224,768]{1,0:T(8,128)(2,1)S(1)}, u32[]{:S(2)}, u32[]{:S(2)}) collective-permute-start(bf16[224,768]{1,0:T(8,128)(2,1)S(1)} %get-tuple-element.45), channel_id=1, source_target_pairs={{4,0},{5,1},{14,2},{7,3},{9,5},{11,7},{12,8},{13,9},{8,10},{15,11}... | collective-permute-start | bytes 1032200 | tf_op jit(solution)/shard_map/ppermute | solution.py:344
  14.4 1.7 %collective-permute-start.3 = (bf16[208,768]{1,0:T(8,128)(2,1)S(1)}, bf16[208,768]{1,0:T(8,128)(2,1)S(1)}, u32[]{:S(2)}, u32[]{:S(2)}) collective-permute-start(bf16[208,768]{1,0:T(8,128)(2,1)S(1)} %collective-permute-done.2.refs_0_), channel_id=1, source_target_pairs={{0,1},{1,0},{2,3},{3,2},{4,5},{5,4},{6,7},{7,6},{8,9},{9,8},{10,11... | collective-permute-start | bytes 958472 | tf_op jit(solution)/shard_map/ppermute | solution.py:347
  22.9 5.7 %copy-start.3 = (f32[768]{0:T(1024)S(1)}, f32[768]{0:T(1024)}, u32[]{:S(2)}) copy-start(f32[768]{0:T(1024)} %param.8) | copy-start | bytes 9220
  22.9 5.8 %copy-start = (bf16[1,768,768]{2,1,0:T(8,128)(2,1)S(1)}, bf16[1,768,768]{2,1,0:T(8,128)(2,1)}, u32[]{:S(2)}) copy-start(bf16[1,768,768]{2,1,0:T(8,128)(2,1)} %param.7) | copy-start | bytes 3538948
  25.1 3.5 %collective-permute-start.4 = (bf16[384,768]{1,0:T(8,128)(2,1)S(1)}, bf16[384,768]{1,0:T(8,128)(2,1)S(1)}, u32[]{:S(2)}, u32[]{:S(2)}) collective-permute-start(bf16[384,768]{1,0:T(8,128)(2,1)S(1)} %collective-permute-done.w_in), channel_id=1, source_target_pairs={{0,1},{1,0},{2,3},{3,2},{4,5},{5,4},{6,7},{7,6},{8,9},{9,8},{10,11... | collective-permute-start | bytes 1769480 | tf_op jit(solution)/shard_map/ppermute | solution.py:347
  25.2 6.5 %collective-permute-start.5 = (f32[2,768]{1,0:T(2,128)S(1)}, f32[2,768]{1,0:T(2,128)S(1)}, u32[]{:S(2)}, u32[]{:S(2)}) collective-permute-start(f32[2,768]{1,0:T(2,128)S(1)} %get-tuple-element.81.refs_0_), channel_id=1, source_target_pairs={{0,8},{8,0},{1,9},{9,1},{16,24},{24,16},{17,25},{25,17}} | collective-permute-start | bytes 18440 | tf_op jit(solution)/shard_map/ppermute | solution.py:389
  32.7 5.5 %collective-permute-start.6 = (f32[6,128]{1,0:T(8,128)S(1)}, f32[6,128]{1,0:T(8,128)S(1)}, u32[]{:S(2)}, u32[]{:S(2)}) collective-permute-start(f32[6,128]{1,0:T(8,128)S(1)} %get-tuple-element.83), channel_id=1, source_target_pairs={{0,2},{1,5},{2,0},{3,7},{4,1},{5,13},{6,3},{7,15},{8,10},{9,14},{1... | collective-permute-start | bytes 9224 | tf_op jit(solution)/shard_map/ppermute | solution.py:344
  35.3 2.9 %collective-permute-start.7 = (f32[6,128]{1,0:T(8,128)S(1)}, f32[6,128]{1,0:T(8,128)S(1)}, u32[]{:S(2)}, u32[]{:S(2)}) collective-permute-start(f32[6,128]{1,0:T(8,128)S(1)} %get-tuple-element.84), channel_id=1, source_target_pairs={{1,7},{3,5},{5,9},{7,11},{9,13},{11,15},{17,23},{19,21},{21,25},{2... | collective-permute-start | bytes 9224 | tf_op jit(solution)/shard_map/ppermute | solution.py:344
  38.2 1.2 %collective-permute-start.8 = (f32[6,128]{1,0:T(8,128)S(1)}, f32[6,128]{1,0:T(8,128)S(1)}, u32[]{:S(2)}, u32[]{:S(2)}) collective-permute-start(f32[6,128]{1,0:T(8,128)S(1)} %add_add_fusion), channel_id=1, source_target_pairs={{0,1},{1,0},{2,3},{3,2},{4,5},{5,4},{6,7},{7,6},{8,9},{9,8},{10,11... | collective-permute-start | bytes 9224 | tf_op jit(solution)/shard_map/ppermute | solution.py:347

commit v4 on v3

--- a/solution.py
+++ b/solution.py
@@ -136,8 +136,9 @@
         y0, y1 = y[:, :rows], y[:, rows:]
         pieces.append(jnp.where(block, jnp.where(real_row, y0, y1), 0.0).astype(BF))
         pieces.append(jnp.where(block, jnp.where(real_row, y1, -y0), 0.0).astype(BF))
-    bands = v[...]
-    return dot(pieces[0], bands) + dot(pieces[2], bands), dot(pieces[1], bands) + dot(pieces[3], bands)
+    left = jnp.concatenate([jnp.concatenate(pieces[0::2], axis=1), jnp.concatenate(pieces[1::2], axis=1)], axis=0)
+    both = dot(left, jnp.concatenate([v[...], v[...]], axis=0))
+    return both[:rows], both[rows:]
 
 
 def sums(c, amp, turned):

time: 40.3 us -> 40.3 us (level)
  transfers between devices with their start and end apart: 9 -> 9, of which waited for: 4 -> 4; matrix products, arithmetic and copies ran while one was open for 3% -> 3% of each run, Pallas kernels for 27% -> 26%
where the time goes in v4:
time: 40.3 us; the launch traced here: 40 us
  starting transfers between devices  15.3 us (38%)
  Pallas kernels  11.6 us (29%)
  waiting for transfers between devices  9.31 us (23%)
  local copies, waits for them, and re-layouts  2.89 us (7%)
  other arithmetic  0.67 us (2%)
    pallas_call x7, Pallas kernels, call(): pl.pallas_call(kernel, out_shape=outs, in_specs=specs, out_specs=[VM] * l...  11.6 us
    ppermute x4, starting transfers between devices, over_cores(): return lax.ppermute(x, ('blk', 'pair'), pairs)  9.32 us
    ppermute x4, waiting for transfers between devices, over_cores(): return lax.ppermute(x, ('blk', 'pair'), pairs)  6.54 us
    ppermute x1, starting transfers between devices, eight_blocks(): xs_in = lax.ppermute(xs, 'blk', SUMS)  3.48 us
    ppermute x3, waiting for transfers between devices, swap(): return lax.ppermute(x, 'pair', [(0, 1), (1, 0)])  2.77 us
    ppermute x1, starting transfers between devices, eight_blocks(): lax.ppermute(lax.dynamic_slice_in_dim(screened[0], member * gh, gh, 0), '...  2.42 us
    dynamic_slice x1, local copies, waits for them, and re-layouts, eight_blocks(): lax.dynamic_slice_in_dim(screened[0], member * gh, gh, 0)  1.11 us
    reshape x1, local copies, waits for them, and re-layouts, eight_blocks(): flat = wavefunc.reshape(kr * nb * 2, planes)  1.09 us
  transfers between devices with their start and end apart: 9, of which 4 were waited for; matrix products, arithmetic and copies ran while one was open for 3% of the time, Pallas kernels for 26%

profile of v4, /device:TPU:0, one launch (start us, length us, event | category | flops | bytes accessed | tf_op | source)
XLA Modules:
  0.0 40.0 jit_solution(2789755222846070776)
XLA Ops:
  0.0 0.0 copy-start.1
  0.0 1.1 %reshape.7.flat = bf16[192,768]{1,0:T(8,128)(2,1)S(1)} reshape(bf16[6,16,2,768]{3,2,1,0:T(2,128)(2,1)} %param.5) | data formatting | bytes 589824 | tf_op jit(solution)/shard_map/reshape | solution.py:369
  1.1 0.0 copy-start.2
  1.1 0.7 %copy-done.2 = f32[6,128]{1,0:T(8,128)S(1)} copy-done((f32[6,128]{1,0:T(8,128)S(1)}, f32[6,128]{1,0:T(8,128)}, u32[]{:S(2)}) %copy-start.2) | copy-done | bytes 3096
  1.8 4.8 %collective-permute-start.2 = (bf16[208,768]{1,0:T(8,128)(2,1)S(1)}, bf16[208,768]{1,0:T(8,128)(2,1)S(1)}, u32[]{:S(2)}, u32[]{:S(2)}) collective-permute-start(bf16[208,768]{1,0:T(8,128)(2,1)S(1)} %get-tuple-element.46.refs_0_), channel_id=1, source_target_pairs={{6,0},{3,1},{0,2},{5,3},{1,4},{13,5},{2,6},{15,7},{10,8},{14,9},{7... | collective-permute-start | bytes 958472 | tf_op jit(solution)/shard_map/ppermute | solution.py:345
  6.7 1.1 %dynamic-slice_bitcast_fusion = bf16[384,768]{1,0:T(8,128)(2,1)S(1)} fusion(bf16[1,768,768]{2,1,0:T(8,128)(2,1)} %param.7, s32[]{:T(128)S(6)} %select_n.3), kind=kLoop, calls=%fused_computation | loop fusion | bytes 1179652 | tf_op jit(solution)/shard_map/dynamic_slice | solution.py:368
  7.8 2.4 %collective-permute-start = (bf16[384,768]{1,0:T(8,128)(2,1)S(1)}, bf16[384,768]{1,0:T(8,128)(2,1)S(1)}, u32[]{:S(2)}, u32[]{:S(2)}) collective-permute-start(bf16[384,768]{1,0:T(8,128)(2,1)S(1)} %dynamic-slice_bitcast_fusion), channel_id=1, source_target_pairs={{0,8},{2,10},{4,6},{1,9},{3,11},{5,7},{16,24},{18,26},{20,22},{17,... | collective-permute-start | bytes 1769480 | tf_op jit(solution)/shard_map/ppermute | solution.py:368
  10.2 1.3 %collective-permute-start.1 = (bf16[224,768]{1,0:T(8,128)(2,1)S(1)}, bf16[224,768]{1,0:T(8,128)(2,1)S(1)}, u32[]{:S(2)}, u32[]{:S(2)}) collective-permute-start(bf16[224,768]{1,0:T(8,128)(2,1)S(1)} %get-tuple-element.45), channel_id=1, source_target_pairs={{4,0},{5,1},{14,2},{7,3},{9,5},{11,7},{12,8},{13,9},{8,10},{15,11}... | collective-permute-start | bytes 1032200 | tf_op jit(solution)/shard_map/ppermute | solution.py:345
  11.5 0.1 pad_add_fusion.who
  11.6 0.0 copy-done.1
  11.6 0.8 %shard_map.55.perm = bf16[768,768]{1,0:T(8,128)(2,1)S(1)} custom-call(s32[2]{0:T(128)S(1)} %pad_add_fusion.who, s32[3,768]{1,0:T(4,128)S(1)} %copy-done.1), custom_call_target="tpu_custom_call" | custom-call | bytes 1188872 | tf_op jit(solution)/shard_map/pallas_call | solution.py:322
  12.4 1.9 %shard_map.57 = (bf16[1,192,768]{2,1,0:T(8,128)(2,1)S(1)}, bf16[1,768,96]{2,1,0:T(8,128)(2,1)S(1)}, bf16[1,96,768]{2,1,0:T(8,128)(2,1)S(1)}, bf16[96,768]{1,0:T(...) custom-call(s32[2]{0:T(128)S(1)} %pad_add_fusion.who, bf16[768,768]{1,0:T(8,128)(2,1)S(1)} %shard_map.55.perm, ...), custom_call_target="tpu_custom_call" | custom-call | bytes 2390024 | tf_op jit(solution)/shard_map/pallas_call | solution.py:322
  14.3 0.0 collective-permute-done.2.refs_0_
  14.4 0.0 collective-permute-start.3
  14.4 1.6 %collective-permute-done.3.refs_1_ = bf16[208,768]{1,0:T(8,128)(2,1)S(1)} collective-permute-done((bf16[208,768]{1,0:T(8,128)(2,1)S(1)}, bf16[208,768]{1,0:T(8,128)(2,1)S(1)}, u32[]{:S(2)}, u32[]{:S(2)}) %collective-permute-start.3) | collective-permute-done | bytes 319520 | tf_op jit(solution)/shard_map/ppermute | solution.py:348
  16.0 2.7 %shard_map.58 = (bf16[2,192,768]{2,1,0:T(8,128)(2,1)S(1)}, bf16[2,768,96]{2,1,0:T(8,128)(2,1)S(1)}, bf16[2,96,768]{2,1,0:T(8,128)(2,1)S(1)}, bf16[192,768]{1,0:T...) custom-call(s32[2]{0:T(128)S(1)} %pad_add_fusion.who, bf16[768,768]{1,0:T(8,128)(2,1)S(1)} %shard_map.55.perm, ...), custom_call_target="tpu_custom_call" | custom-call | tf_op jit(solution)/shard_map/pallas_call | solution.py:322
  18.7 4.2 %collective-permute-done.1.msg = bf16[224,768]{1,0:T(8,128)(2,1)S(1)} collective-permute-done((bf16[224,768]{1,0:T(8,128)(2,1)S(1)}, bf16[224,768]{1,0:T(8,128)(2,1)S(1)}, u32[]{:S(2)}, u32[]{:S(2)}) %collective-permute-start.1) | collective-permute-done | bytes 344096 | tf_op jit(solution)/shard_map/ppermute | solution.py:345
  22.9 0.0 copy-start.3
  22.9 0.0 copy-start
  22.9 2.2 %shard_map.59 = (bf16[2,192,768]{2,1,0:T(8,128)(2,1)S(1)}, bf16[2,768,96]{2,1,0:T(8,128)(2,1)S(1)}, bf16[2,96,768]{2,1,0:T(8,128)(2,1)S(1)}, bf16[2,96,768]{2,1,...) custom-call(s32[2]{0:T(128)S(1)} %pad_add_fusion.who, bf16[768,768]{1,0:T(8,128)(2,1)S(1)} %shard_map.55.perm, ...), custom_call_target="tpu_custom_call" | custom-call | bytes 5959688 | tf_op jit(solution)/shard_map/pallas_call | solution.py:322
  25.0 0.0 collective-permute-done.w_in
  25.0 0.1 collective-permute-start.4
  25.1 3.5 %collective-permute-start.5 = (f32[2,768]{1,0:T(2,128)S(1)}, f32[2,768]{1,0:T(2,128)S(1)}, u32[]{:S(2)}, u32[]{:S(2)}) collective-permute-start(f32[2,768]{1,0:T(2,128)S(1)} %get-tuple-element.81.refs_0_), channel_id=1, source_target_pairs={{0,8},{8,0},{1,9},{9,1},{16,24},{24,16},{17,25},{25,17}} | collective-permute-start | bytes 18440 | tf_op jit(solution)/shard_map/ppermute | solution.py:390
  28.6 0.0 copy-done.3
  28.6 0.0 collective-permute-done.4.w_swapped
  28.6 0.0 copy-done
  28.6 3.0 %shard_map.60.d_ref = f32[2,96,96]{2,1,0:T(8,128)S(1)} custom-call(s32[2]{0:T(128)S(1)} %pad_add_fusion.who, bf16[768,768]{1,0:T(8,128)(2,1)S(1)} %bitcast.5, bf16[384,768]{1,0:T(8,128)(2,1)S(1)} %collective-permute-done.w_in, bf16[384,768]{1,0:T(8,128)(2,1)S(1)} %collective-permute-done.4.w_swapped, bf16[2,192,768]{2,1,0:T(8,128)(2,1)S(1)} %get-tuple-element.76.ap, ...), custom_call_target="tpu_custom_call" | custom-call | bytes 4202504 | tf_op jit(solution)/shard_map/pallas_call | solution.py:322
  31.7 0.0 collective-permute-done.5.refs_1_
  31.7 1.0 %shard_map.61 = (f32[6,128]{1,0:T(8,128)S(1)}, f32[6,128]{1,0:T(8,128)S(1)}, f32[6,128]{1,0:T(8,128)S(1)}) custom-call(s32[2]{0:T(128)S(1)} %pad_add_fusion.who, f32[2,96,96]{2,1,0:T(8,128)S(1)} %shard_map.60.d_ref, bf16[2,96,768]{2,1,0:T(8,128)(2,1)S(1)} %get-tuple-element.78.v, bf16[2,96,768]{2,1,0:T(8,128)(2,1)S(1)} %get-tuple-element.79.ca, ...), custom_call_target="tpu_custom_call" | custom-call | bytes 983048 | tf_op jit(solution)/shard_map/pallas_call | solution.py:322
  32.7 2.5 %collective-permute-start.6 = (f32[6,128]{1,0:T(8,128)S(1)}, f32[6,128]{1,0:T(8,128)S(1)}, u32[]{:S(2)}, u32[]{:S(2)}) collective-permute-start(f32[6,128]{1,0:T(8,128)S(1)} %get-tuple-element.83), channel_id=1, source_target_pairs={{0,2},{1,5},{2,0},{3,7},{4,1},{5,13},{6,3},{7,15},{8,10},{9,14},{1... | collective-permute-start | bytes 9224 | tf_op jit(solution)/shard_map/ppermute | solution.py:345
  35.3 0.7 %collective-permute-start.7 = (f32[6,128]{1,0:T(8,128)S(1)}, f32[6,128]{1,0:T(8,128)S(1)}, u32[]{:S(2)}, u32[]{:S(2)}) collective-permute-start(f32[6,128]{1,0:T(8,128)S(1)} %get-tuple-element.84), channel_id=1, source_target_pairs={{1,7},{3,5},{5,9},{7,11},{9,13},{11,15},{17,23},{19,21},{21,25},{2... | collective-permute-start | bytes 9224 | tf_op jit(solution)/shard_map/ppermute | solution.py:345
  35.9 2.3 %collective-permute-done.6 = f32[6,128]{1,0:T(8,128)S(1)} collective-permute-done((f32[6,128]{1,0:T(8,128)S(1)}, f32[6,128]{1,0:T(8,128)S(1)}, u32[]{:S(2)}, u32[]{:S(2)}) %collective-permute-start.6) | collective-permute-done | bytes 3104 | tf_op jit(solution)/shard_map/ppermute | solution.py:345
  38.2 0.0 collective-permute-done.7
  38.2 0.0 collective-permute-start.8
  38.2 1.2 %collective-permute-done.8 = f32[6,128]{1,0:T(8,128)S(1)} collective-permute-done((f32[6,128]{1,0:T(8,128)S(1)}, f32[6,128]{1,0:T(8,128)S(1)}, u32[]{:S(2)}, u32[]{:S(2)}) %collective-permute-start.8) | collective-permute-done | bytes 3104 | tf_op jit(solution)/shard_map/ppermute | solution.py:348
  39.4 0.6 %add.15 = f32[6,128]{1,0:T(8,128)} add(f32[6,128]{1,0:T(8,128)S(1)} %add_add_fusion, f32[6,128]{1,0:T(8,128)S(1)} %collective-permute-done.8) | non-fusion elementwise | flops 768 | bytes 9216 | tf_op jit(solution)/shard_map/add | solution.py:404
  (3 shorter events, 0.1 us)
Async XLA Ops:
  0.0 11.6 %copy-start.1 = (s32[3,768]{1,0:T(4,128)S(1)}, s32[3,768]{1,0:T(4,128)}, u32[]{:S(2)}) copy-start(s32[3,768]{1,0:T(4,128)} %umk.1) | copy-start | bytes 27652
  1.1 0.7 %copy-start.2 = (f32[6,128]{1,0:T(8,128)S(1)}, f32[6,128]{1,0:T(8,128)}, u32[]{:S(2)}) copy-start(f32[6,128]{1,0:T(8,128)} %hay.1) | copy-start | bytes 9220
  1.8 12.5 %collective-permute-start.2 = (bf16[208,768]{1,0:T(8,128)(2,1)S(1)}, bf16[208,768]{1,0:T(8,128)(2,1)S(1)}, u32[]{:S(2)}, u32[]{:S(2)}) collective-permute-start(bf16[208,768]{1,0:T(8,128)(2,1)S(1)} %get-tuple-element.46.refs_0_), channel_id=1, source_target_pairs={{6,0},{3,1},{0,2},{5,3},{1,4},{13,5},{2,6},{15,7},{10,8},{14,9},{7... | collective-permute-start | bytes 958472 | tf_op jit(solution)/shard_map/ppermute | solution.py:345
  7.8 17.2 %collective-permute-start = (bf16[384,768]{1,0:T(8,128)(2,1)S(1)}, bf16[384,768]{1,0:T(8,128)(2,1)S(1)}, u32[]{:S(2)}, u32[]{:S(2)}) collective-permute-start(bf16[384,768]{1,0:T(8,128)(2,1)S(1)} %dynamic-slice_bitcast_fusion), channel_id=1, source_target_pairs={{0,8},{2,10},{4,6},{1,9},{3,11},{5,7},{16,24},{18,26},{20,22},{17,... | collective-permute-start | bytes 1769480 | tf_op jit(solution)/shard_map/ppermute | solution.py:368
  10.2 12.6 %collective-permute-start.1 = (bf16[224,768]{1,0:T(8,128)(2,1)S(1)}, bf16[224,768]{1,0:T(8,128)(2,1)S(1)}, u32[]{:S(2)}, u32[]{:S(2)}) collective-permute-start(bf16[224,768]{1,0:T(8,128)(2,1)S(1)} %get-tuple-element.45), channel_id=1, source_target_pairs={{4,0},{5,1},{14,2},{7,3},{9,5},{11,7},{12,8},{13,9},{8,10},{15,11}... | collective-permute-start | bytes 1032200 | tf_op jit(solution)/shard_map/ppermute | solution.py:345
  14.4 1.7 %collective-permute-start.3 = (bf16[208,768]{1,0:T(8,128)(2,1)S(1)}, bf16[208,768]{1,0:T(8,128)(2,1)S(1)}, u32[]{:S(2)}, u32[]{:S(2)}) collective-permute-start(bf16[208,768]{1,0:T(8,128)(2,1)S(1)} %collective-permute-done.2.refs_0_), channel_id=1, source_target_pairs={{0,1},{1,0},{2,3},{3,2},{4,5},{5,4},{6,7},{7,6},{8,9},{9,8},{10,11... | collective-permute-start | bytes 958472 | tf_op jit(solution)/shard_map/ppermute | solution.py:348
  22.9 5.7 %copy-start.3 = (f32[768]{0:T(1024)S(1)}, f32[768]{0:T(1024)}, u32[]{:S(2)}) copy-start(f32[768]{0:T(1024)} %param.8) | copy-start | bytes 9220
  22.9 5.8 %copy-start = (bf16[1,768,768]{2,1,0:T(8,128)(2,1)S(1)}, bf16[1,768,768]{2,1,0:T(8,128)(2,1)}, u32[]{:S(2)}) copy-start(bf16[1,768,768]{2,1,0:T(8,128)(2,1)} %param.7) | copy-start | bytes 3538948
  25.0 3.6 %collective-permute-start.4 = (bf16[384,768]{1,0:T(8,128)(2,1)S(1)}, bf16[384,768]{1,0:T(8,128)(2,1)S(1)}, u32[]{:S(2)}, u32[]{:S(2)}) collective-permute-start(bf16[384,768]{1,0:T(8,128)(2,1)S(1)} %collective-permute-done.w_in), channel_id=1, source_target_pairs={{0,1},{1,0},{2,3},{3,2},{4,5},{5,4},{6,7},{7,6},{8,9},{9,8},{10,11... | collective-permute-start | bytes 1769480 | tf_op jit(solution)/shard_map/ppermute | solution.py:348
  25.1 6.6 %collective-permute-start.5 = (f32[2,768]{1,0:T(2,128)S(1)}, f32[2,768]{1,0:T(2,128)S(1)}, u32[]{:S(2)}, u32[]{:S(2)}) collective-permute-start(f32[2,768]{1,0:T(2,128)S(1)} %get-tuple-element.81.refs_0_), channel_id=1, source_target_pairs={{0,8},{8,0},{1,9},{9,1},{16,24},{24,16},{17,25},{25,17}} | collective-permute-start | bytes 18440 | tf_op jit(solution)/shard_map/ppermute | solution.py:390
  32.7 5.5 %collective-permute-start.6 = (f32[6,128]{1,0:T(8,128)S(1)}, f32[6,128]{1,0:T(8,128)S(1)}, u32[]{:S(2)}, u32[]{:S(2)}) collective-permute-start(f32[6,128]{1,0:T(8,128)S(1)} %get-tuple-element.83), channel_id=1, source_target_pairs={{0,2},{1,5},{2,0},{3,7},{4,1},{5,13},{6,3},{7,15},{8,10},{9,14},{1... | collective-permute-start | bytes 9224 | tf_op jit(solution)/shard_map/ppermute | solution.py:345
  35.3 3.0 %collective-permute-start.7 = (f32[6,128]{1,0:T(8,128)S(1)}, f32[6,128]{1,0:T(8,128)S(1)}, u32[]{:S(2)}, u32[]{:S(2)}) collective-permute-start(f32[6,128]{1,0:T(8,128)S(1)} %get-tuple-element.84), channel_id=1, source_target_pairs={{1,7},{3,5},{5,9},{7,11},{9,13},{11,15},{17,23},{19,21},{21,25},{2... | collective-permute-start | bytes 9224 | tf_op jit(solution)/shard_map/ppermute | solution.py:345
  38.2 1.2 %collective-permute-start.8 = (f32[6,128]{1,0:T(8,128)S(1)}, f32[6,128]{1,0:T(8,128)S(1)}, u32[]{:S(2)}, u32[]{:S(2)}) collective-permute-start(f32[6,128]{1,0:T(8,128)S(1)} %add_add_fusion), channel_id=1, source_target_pairs={{0,1},{1,0},{2,3},{3,2},{4,5},{5,4},{6,7},{7,6},{8,9},{9,8},{10,11... | collective-permute-start | bytes 9224 | tf_op jit(solution)/shard_map/ppermute | solution.py:348
